TPU v7x, 32 devices: a whole 2x2x4 slice. The times are simulated.
32 devices in a mesh: dp: 4 (over y, core), proto: 8 (over z, x).
Axes of the slice: x: 2, y: 2, z: 4, core: 2. Of those that a mesh axis runs over, the one named last changes fastest.
Arguments:
- student_cls: bfloat16 [32, 1536], P(('dp', 'proto')), may hold values from -6 to 6
- student_patches: bfloat16 [32, 256, 1536], P(('dp', 'proto')), may hold values from -6 to 6
- teacher_cls: bfloat16 [32, 1536], P(('dp', 'proto')), may hold values from -6 to 6
- teacher_patches: bfloat16 [32, 256, 1536], P(('dp', 'proto')), may hold values from -6 to 6
- mask_index: int32 [32, 31], P(('dp', 'proto')), may hold values from 0 to 255, as said below
- crop_pair: int32 [32], P(('dp', 'proto')), may hold values from 0 to 7, as said below
- center: float32 [2, 65536], P(None, 'proto'), may hold values from -0.3 to 0.3
- student_w1: bfloat16 [1536, 2048], P('dp', 'proto'), may hold values from -0.15625 to 0.15625
- student_w2: bfloat16 [2048, 256], P('proto'), may hold values from -0.06970923 to 0.06970923
- teacher_w1: bfloat16 [1536, 2048], P('dp', 'proto'), may hold values from -0.15625 to 0.15625
- teacher_w2: bfloat16 [2048, 256], P('proto'), may hold values from -0.06970923 to 0.06970923
- student_proto: float32 [256, 65536], P(None, 'proto'), may hold values from -0.39 to 0.39
- teacher_proto: float32 [256, 65536], P(None, 'proto'), may hold values from -0.39 to 0.39
Outputs:
- loss_value: float32 [4], P('dp')
- grad_w1: float32 [1536, 2048], P('dp', 'proto')
- grad_w2: float32 [2048, 256], P('proto')
- grad_proto: float32 [256, 65536], P('dp', 'proto')
Inputs may be any that keep to these rules, and one draw needn't show every extreme that they name: `mask_index`: the 31 indices of one crop are distinct. Within each dp index's 8 crops, crop_pair pairs crops: crop_pair[crop_pair[c]] = c and crop_pair[c] != c.
All inputs are finite; a program needn't handle non-finite values.
Results may differ from a plain program's by a relative error of at most 0.006.
Values may be sent and summed in bfloat16 or wider, within the bound.
A program may use at most 128 MiB of HBM per device.

v0:
```python
import jax
import jax.numpy as jnp
from jax import lax
from jax.sharding import PartitionSpec as P

epsilon = 1e-06
teacher_temp = 0.07
student_temp = 0.1
loss_scale = 1048576.0


def select_rows(cls_tokens, patches, mask_index):
    picked = jax.vmap(lambda patch_set, index_set: patch_set[index_set])(patches, mask_index)
    joined = jnp.concatenate([cls_tokens[:, None, :], picked], axis=1)
    return joined.reshape(-1, cls_tokens.shape[-1])


def normalize_rows(bottle):
    inverse = lax.rsqrt(jnp.sum(bottle * bottle, axis=-1, keepdims=True) + epsilon)
    return (bottle * inverse, inverse)


def normalize_columns(proto):
    inverse = lax.rsqrt(jnp.sum(proto * proto, axis=0, keepdims=True) + epsilon)
    return (proto * inverse, inverse)


def gelu_grad(preact):
    normal_cdf = 0.5 * (1.0 + lax.erf(preact * 0.7071067811865476))
    normal_pdf = jnp.exp(-0.5 * preact * preact) * 0.3989422804014327
    return normal_cdf + preact * normal_pdf


def contract_rows(left, right):
    return lax.dot_general(
        left, right, (((0,), (0,)), ((), ())), preferred_element_type=jnp.float32
    )


def shards(
    student_cls,
    student_patches,
    teacher_cls,
    teacher_patches,
    mask_index,
    crop_pair,
    center,
    student_w1,
    student_w2,
    teacher_w1,
    teacher_w2,
    student_proto,
    teacher_proto,
):
    row_span = mask_index.shape[1] + 1
    masked_count = mask_index.shape[1]
    local_crops = student_cls.shape[0]
    proto_ways = lax.axis_size("proto")
    data_ways = lax.axis_size("dp")
    crop_group = local_crops * proto_ways
    group_rows = crop_group * row_span
    crops_total = crop_group * data_ways
    bottleneck = student_w2.shape[1]
    rows_student = select_rows(student_cls, student_patches, mask_index)
    rows_teacher = select_rows(teacher_cls, teacher_patches, mask_index)
    stacked_w1 = jnp.stack([student_w1, teacher_w1])
    column_w1 = lax.all_gather(stacked_w1, "dp", axis=1, tiled=True)
    teacher_all = lax.all_gather(rows_teacher, "proto", axis=0, tiled=True)
    teacher_pre = jnp.dot(teacher_all, column_w1[1], preferred_element_type=jnp.float32)
    teacher_hidden = jax.nn.gelu(teacher_pre, approximate=False).astype(jnp.bfloat16)
    row_block = teacher_hidden
    bottle_t = lax.psum_scatter(
        jnp.dot(row_block, teacher_w2, preferred_element_type=jnp.float32),
        "proto",
        scatter_dimension=0,
        tiled=True,
    )
    preact = jnp.dot(
        rows_student,
        lax.all_gather(column_w1[0], "proto", axis=1, tiled=True),
        preferred_element_type=jnp.float32,
    )
    hidden = jax.nn.gelu(preact, approximate=False).astype(jnp.bfloat16)
    full_w2 = lax.all_gather(student_w2, "proto", axis=0, tiled=True)
    bottle_s = jnp.dot(hidden, full_w2, preferred_element_type=jnp.float32)
    unit_s, inverse_s = normalize_rows(bottle_s)
    unit_t, _ = normalize_rows(bottle_t)
    packed = jnp.concatenate([unit_s, unit_t], axis=1).astype(jnp.bfloat16)
    all_units, all_pairs = (
        lax.all_gather(packed, "proto", axis=0, tiled=True),
        lax.all_gather(crop_pair, "proto", axis=0, tiled=True),
    )
    index_rows = jnp.arange(group_rows, dtype=jnp.int32)
    is_cls = index_rows % row_span == 0
    crop_local = index_rows // row_span
    match_table = crop_local[:, None] == jnp.arange(crop_group, dtype=jnp.int32)[None, :]
    partner_crop = jnp.sum(jnp.where(match_table, all_pairs[None, :], 0), axis=1)
    target = jnp.where(is_cls, partner_crop * row_span, index_rows)
    group_s = all_units[:, :bottleneck]
    aligned = jnp.take(all_units[:, bottleneck:], target, axis=0)
    proto_unit, col_inverse = normalize_columns(student_proto)
    teacher_unit, _ = normalize_columns(teacher_proto)
    proto_s_b = proto_unit.astype(jnp.bfloat16)
    proto_t_b = teacher_unit.astype(jnp.bfloat16)
    shift = jnp.where(is_cls[:, None], center[0][None, :], center[1][None, :])
    logit_s = jnp.dot(group_s, proto_s_b, preferred_element_type=jnp.float32) / student_temp
    logit_t = (
        jnp.dot(aligned, proto_t_b, preferred_element_type=jnp.float32) - shift
    ) / teacher_temp
    total_t, total_s = lax.psum(
        (jnp.sum(jnp.exp(logit_t), axis=1), jnp.sum(jnp.exp(logit_s), axis=1)), "proto"
    )
    cross_term = lax.psum(jnp.sum(jnp.exp(logit_t) / total_t[:, None] * logit_s, axis=1), "proto")
    weights = jnp.where(is_cls, 1.0 / crops_total, 1.0 / (crops_total * masked_count)).astype(
        jnp.float32
    )
    row_loss = jnp.log(total_s) - cross_term
    loss_value = (jnp.sum(weights * row_loss) * data_ways).reshape(1)
    factor = loss_scale / student_temp * weights
    dscore = (
        factor[:, None]
        * (jnp.exp(logit_s) / total_s[:, None] - jnp.exp(logit_t) / total_t[:, None])
    ).astype(jnp.bfloat16)
    row_block = dscore
    grad_units = lax.psum_scatter(
        lax.dot_general(
            row_block, proto_s_b, (((1,), (1,)), ((), ())), preferred_element_type=jnp.float32
        ),
        "proto",
        scatter_dimension=0,
        tiled=True,
    )
    grad_cols = contract_rows(group_s, dscore)
    projected = col_inverse * (
        grad_cols - proto_unit * jnp.sum(proto_unit * grad_cols, axis=0, keepdims=True)
    )
    grad_proto = lax.psum_scatter(projected, "dp", scatter_dimension=0, tiled=True)
    grad_z = (
        inverse_s * (grad_units - unit_s * jnp.sum(unit_s * grad_units, axis=1, keepdims=True))
    ).astype(jnp.bfloat16)
    grad_hidden = lax.dot_general(
        grad_z, full_w2, (((1,), (1,)), ((), ())), preferred_element_type=jnp.float32
    )
    grad_pre = (grad_hidden * gelu_grad(preact)).astype(jnp.bfloat16)
    row_block = rows_student
    partial_w1 = lax.psum_scatter(
        contract_rows(row_block, grad_pre), "dp", scatter_dimension=0, tiled=True
    )
    grad_w1 = lax.psum_scatter(partial_w1, "proto", scatter_dimension=1, tiled=True)
    row_block = hidden
    partial_w2 = lax.psum_scatter(
        contract_rows(row_block, grad_z), "proto", scatter_dimension=0, tiled=True
    )
    grad_w2 = lax.psum(partial_w2, "dp")
    return (loss_value, grad_w1, grad_w2, grad_proto)


def solution(mesh):
    placed = (
        P(("dp", "proto"), None),
        P(("dp", "proto"), None, None),
        P(("dp", "proto"), None),
        P(("dp", "proto"), None, None),
        P(("dp", "proto"), None),
        P(("dp", "proto")),
        P(None, "proto"),
        P("dp", "proto"),
        P("proto", None),
        P("dp", "proto"),
        P("proto", None),
        P(None, "proto"),
        P(None, "proto"),
    )
    return jax.shard_map(
        shards,
        mesh=mesh,
        in_specs=placed,
        out_specs=(P("dp"), P("dp", "proto"), P("proto", None), P("dp", "proto")),
        check_vma=False,
    )
```

profile of v0, /device:TPU:0, one launch (start us, length us, event | category | flops | bytes accessed | tf_op | source)
XLA Modules:
  0.0 786.4 jit_solution(17128747420710999753)
XLA Ops:
  11.5 33.9 %all-gather.1 = bf16[1,256,1536]{2,1,0:T(8,128)(2,1)S(1)} all-gather(bf16[1,32,1536]{2,1,0:T(8,128)(2,1)S(1)} %pad_maximum_fusion.1), channel_id=3, replica_groups=mesh['dp'=4,'proto'=8] {'proto'}, dimensions={1}, use_global_device_ids=true | all-gather | bytes 884736 | tf_op jit(solution)/shard_map/all_gather | solution.py:68
  52.2 10.8 %all-reduce = s32[8]{0:T(128)S(1)} all-reduce(s32[8]{0:T(128)S(1)} %dynamic-update-slice), channel_id=1, replica_groups=mesh['dp'=4,'proto'=8] {'proto'}, use_global_device_ids=true, to_apply=%add | all-reduce | flops 8 | bytes 64
  63.2 4.1 multiply_reduce_fusion.2
  68.3 4.1 multiply_reduce_fusion.3
  72.4 38.4 %reduce-scatter.7.cloned.1.call-done = f32[32,256]{1,0:T(8,128)} async-done(((f32[256,256]{1,0:T(8,128)}), f32[32,256]{1,0:T(8,128)}) %reduce-scatter.7.cloned.1.call-update) | async-done | bytes 32784 | tf_op jit(solution)/shard_map/reduce_scatter | solution.py:72
  112.6 99.9 %all-gather.10.cloned.1.call-done = bf16[1,1536,2048]{2,1,0:T(8,128)(2,1)} async-done(((bf16[1,1536,256]{2,1,0:T(8,128)(2,1)}), bf16[1,1536,2048]{2,1,0:T(8,128)(2,1)}) %all-gather.10.cloned.1.call-update) | async-done | bytes 6291472 | tf_op jit(solution)/shard_map/all_gather | solution.py:80
  212.5 4.5 fusion.12
  217.0 35.9 %all-gather.8.cloned.1.call-done = bf16[2048,256]{1,0:T(8,128)(2,1)} async-done(((bf16[256,256]{1,0:T(8,128)(2,1)}), bf16[2048,256]{1,0:T(8,128)(2,1)}) %all-gather.8.cloned.1.call-update) | async-done | bytes 1048592 | tf_op jit(solution)/shard_map/all_gather | solution.py:84
  254.6 30.8 %all_gather.22 = bf16[256,512]{1,0:T(8,128)(2,1)S(1)} all-gather(bf16[32,512]{1,0:T(8,128)(2,1)S(1)} %pad_maximum_fusion.2), channel_id=1, replica_groups=mesh['dp'=4,'proto'=8] {'proto'}, dimensions={0}, use_global_device_ids=true | all-gather | bytes 294912 | tf_op jit(solution)/shard_map/all_gather | solution.py:90
  286.5 8.8 %fusion.128 = (f32[256]{0:T(256)S(1)}, f32[256,8192]{1,0:T(8,128)}) fusion(f32[8192]{0:T(1024)S(1)} %bitcast.56, f32[8192]{0:T(1024)S(1)} %bitcast.55, pred[256]{0:T(512)(128)(4,1)S(1)} %fusion.87, f32[256,8192]{1,0:T(8,128)} %param.25, f32[8192]{0:T(1024)S(1)} %add_rsqrt_fusion, bf16[256,256]{1,0:T(8,128)(2,1)S(1)} %gather_fusion, ...), kind=kOutput, calls=%fused_computation.192 | convolution fusion | flops 1086390016 | bytes 17008128 | tf_op jit(solution)/shard_map/dot_general | solution.py:108
  295.3 19.2 %psum.29 = f32[256]{0:T(256)S(1)} all-reduce(f32[256]{0:T(256)S(1)} %get-tuple-element.14), channel_id=1, replica_groups=mesh['dp'=4,'proto'=8] {'proto'}, use_global_device_ids=true, to_apply=%region_9.10 | all-reduce | flops 256 | bytes 2048 | tf_op jit(solution)/shard_map/psum | solution.py:110
  314.5 10.1 %exponential_reduce_fusion = (f32[256]{0:T(256)S(1)}, f32[256]{0:T(256)S(1)}, f32[256,8192]{1,0:T(8,128)}) fusion(f32[256,8192]{1,0:T(8,128)} %get-tuple-element.15, f32[256]{0:T(256)S(1)} %psum.29, f32[256,8192]{1,0:T(8,128)} %param.24, f32[8192]{0:T(1024)S(1)} %add_rsqrt_fusion.1, bf16[256,512]{1,0:T(8,128)(2,1)S(1)} %all_gather.22), kind=kOutput, calls=%fused_computation.14 | convolution fusion | flops 1088421376 | bytes 25332736 | tf_op jit(solution)/shard_map/dot_general | solution.py:106
  324.6 17.3 %all-reduce.1 = (f32[256]{0:T(256)S(1)}, f32[256]{0:T(256)S(1)}) all-reduce(f32[256]{0:T(256)S(1)} %get-tuple-element.5, f32[256]{0:T(256)S(1)} %get-tuple-element.4), channel_id=1, replica_groups=mesh['dp'=4,'proto'=8] {'proto'}, use_global_device_ids=true, to_apply=%region_11.12 | all-reduce | flops 512 | bytes 4096 | tf_op jit(solution)/shard_map/psum | solution.py:113
  341.9 7.2 multiply_convert_fusion
  351.0 5.6 fusion.6
  356.7 60.0 %reduce-scatter.9.cloned.1.call-done = f32[32,256]{1,0:T(8,128)} async-done(((f32[256,256]{1,0:T(8,128)}), f32[32,256]{1,0:T(8,128)}) %reduce-scatter.9.cloned.1.call-update) | async-done | bytes 32784 | tf_op jit(solution)/shard_map/reduce_scatter | solution.py:125
  420.4 6.6 fusion.7
  427.1 9.5 %multiply_reduce_fusion = (f32[8192]{0:T(1024)S(1)}, f32[256,8192]{1,0:T(8,128)}) fusion(f32[256,8192]{1,0:T(8,128)} %param.24, f32[8192]{0:T(1024)S(1)} %add_rsqrt_fusion.1, bf16[256,8192]{1,0:T(8,128)(2,1)} %copy-done.2, bf16[256,512]{1,0:T(8,128)(2,1)S(1)} %all_gather.22), kind=kOutput, calls=%fused_computation.8 | convolution fusion | flops 1080025088 | bytes 21168128 | tf_op jit(solution)/shard_map/dot_general | solution.py:35
  436.6 50.8 %reduce-scatter.15.cloned.1.call-done = f32[256,256]{1,0:T(8,128)} async-done(((f32[2048,256]{1,0:T(8,128)}), f32[256,256]{1,0:T(8,128)}) %reduce-scatter.15.cloned.1.call-update) | async-done | bytes 262160 | tf_op jit(solution)/shard_map/reduce_scatter | solution.py:151
  487.5 12.4 %subtract_multiply_fusion = f32[256,8192]{1,0:T(8,128)} fusion(f32[256,8192]{1,0:T(8,128)} %get-tuple-element.18, f32[256,8192]{1,0:T(8,128)} %param.24, f32[8192]{0:T(1024)S(1)} %get-tuple-element.17, f32[8192]{0:T(1024)S(1)} %add_rsqrt_fusion.1), kind=kLoop, calls=%fused_computation.7 | loop fusion | flops 8388608 | bytes 25231360 | tf_op jit(solution)/shard_map/mul | solution.py:134
  500.0 88.1 %reduce-scatter.11.cloned.1.call-done = f32[384,2048]{1,0:T(8,128)} async-done(((f32[1536,2048]{1,0:T(8,128)}), f32[384,2048]{1,0:T(8,128)}) %reduce-scatter.11.cloned.1.call-update) | async-done | bytes 3145744 | tf_op jit(solution)/shard_map/reduce_scatter | solution.py:146
  589.4 33.1 %all-reduce.4.cloned.1.call-done = f32[256,256]{1,0:T(8,128)} async-done(((f32[256,256]{1,0:T(8,128)}), f32[256,256]{1,0:T(8,128)}) %all-reduce.4.cloned.1.call-update) | async-done | bytes 262160 | tf_op jit(solution)/shard_map/psum | solution.py:154
  622.5 75.1 %reduce-scatter.17.cloned.1.call-done = f32[64,8192]{1,0:T(8,128)} async-done(((f32[256,8192]{1,0:T(8,128)}), f32[64,8192]{1,0:T(8,128)}) %reduce-scatter.17.cloned.1.call-update) | async-done | bytes 2097168 | tf_op jit(solution)/shard_map/reduce_scatter | solution.py:137
  697.6 79.2 %reduce-scatter.13.cloned.1.call-done = f32[384,256]{1,0:T(8,128)} async-done(((f32[384,2048]{1,0:T(8,128)}), f32[384,256]{1,0:T(8,128)}) %reduce-scatter.13.cloned.1.call-update) | async-done | bytes 393232 | tf_op jit(solution)/shard_map/reduce_scatter | solution.py:149
  (76 shorter events, 24.2 us)
Async XLA Ops:
  7.2 2.7 copy-start
  7.2 43.6 %copy-start.8 = (u32[32]{0:T(128)S(1)}, u32[32]{0:T(128)}, u32[]{:S(2)}) copy-start(u32[32]{0:T(128)} %constant.201) | copy-start | bytes 388
  7.2 55.9 %copy-start.6 = (f32[2,8192]{1,0:T(2,128)S(1)}, f32[2,8192]{1,0:T(2,128)}, u32[]{:S(2)}) copy-start(f32[2,8192]{1,0:T(2,128)} %param.19) | copy-start | bytes 196612
  7.2 38.2 %all-gather.6.cloned.1.call-start = ((), (), s32[]{:S(2)}) async-start(), calls=%async_computation.6 | async-start | bytes 1966080 | tf_op jit(solution)/shard_map/all_gather | solution.py:67
  9.1 101.7 %reduce-scatter.7.cloned.1.call-start = ((), (), s32[]{:S(2)}) async-start(), calls=%async_computation.8 | async-start | bytes 294912 | tf_op jit(solution)/shard_map/reduce_scatter | solution.py:72
  45.4 21.9 %copy-start.4 = (bf16[1,256,1536]{2,1,0:T(8,128)(2,1)S(1)}, bf16[1,256,1536]{2,1,0:T(8,128)(2,1)}, u32[]{:S(2)}) copy-start(bf16[1,256,1536]{2,1,0:T(8,128)(2,1)} %param.14) | copy-start | bytes 2359300
  45.4 3.1 copy-start.5
  48.5 164.0 %all-gather.10.cloned.1.call-start = ((), (), s32[]{:S(2)}) async-start(), calls=%async_computation.15 | async-start | bytes 7077888 | tf_op jit(solution)/shard_map/all_gather | solution.py:80
  49.5 203.3 %all-gather.8.cloned.1.call-start = ((), (), s32[]{:S(2)}) async-start(), calls=%async_computation.7 | async-start | bytes 1179648 | tf_op jit(solution)/shard_map/all_gather | solution.py:84
  50.1 366.6 %reduce-scatter.9.cloned.1.call-start = ((), (), s32[]{:S(2)}) async-start(), calls=%async_computation.9 | async-start | bytes 294912 | tf_op jit(solution)/shard_map/reduce_scatter | solution.py:125
  63.2 149.3 %copy-start.7 = (bf16[1,1536]{1,0:T(2,128)(2,1)S(1)}, bf16[1,1536]{1,0:T(2,128)(2,1)}, u32[]{:S(2)}) copy-start(bf16[1,1536]{1,0:T(2,128)(2,1)} %param.13) | copy-start | bytes 9220
  349.1 2.0 copy-start.2
  351.0 69.3 %copy-start.3 = (bf16[2048,256]{1,0:T(8,128)(2,1)S(1)}, bf16[2048,256]{1,0:T(8,128)(2,1)}, u32[]{:S(2)}) copy-start(bf16[2048,256]{1,0:T(8,128)(2,1)} %all-gather.8.cloned.1.call-done) | copy-start | bytes 3145732
  356.7 130.8 %reduce-scatter.15.cloned.1.call-start = ((), (), s32[]{:S(2)}) async-start(), calls=%async_computation.12 | async-start | bytes 2359296 | tf_op jit(solution)/shard_map/reduce_scatter | solution.py:151
  420.3 167.8 %reduce-scatter.11.cloned.1.call-start = ((), (), s32[]{:S(2)}) async-start(), calls=%async_computation.10 | async-start | bytes 15728640 | tf_op jit(solution)/shard_map/reduce_scatter | solution.py:146
  427.1 195.4 %all-reduce.4.cloned.1.call-start = ((), (), s32[]{:S(2)}) async-start(), calls=%async_computation.13 | async-start | bytes 524288 | tf_op jit(solution)/shard_map/psum | solution.py:154
  487.4 210.1 %reduce-scatter.17.cloned.1.call-start = ((), (), s32[]{:S(2)}) async-start(), calls=%async_computation.14 | async-start | bytes 10485760 | tf_op jit(solution)/shard_map/reduce_scatter | solution.py:137
  487.5 290.9 %copy-start.1 = (bf16[1,256,1536]{2,1,0:T(8,128)(2,1)S(1)}, bf16[1,256,1536]{2,1,0:T(8,128)(2,1)}, u32[]{:S(2)}) copy-start(bf16[1,256,1536]{2,1,0:T(8,128)(2,1)} %param.16) | copy-start | bytes 2359300
  499.9 276.8 %reduce-scatter.13.cloned.1.call-start = ((), (), s32[]{:S(2)}) async-start(), calls=%async_computation.11 | async-start | bytes 3538944 | tf_op jit(solution)/shard_map/reduce_scatter | solution.py:149
Sparse Core Ops, SparseCore 0:
  10.2 22.3 all-gather.5
  48.6 62.1 reduce-scatter.6
  113.5 98.9 all-gather.9
  214.5 38.3 all-gather.7
  356.8 59.8 reduce-scatter.8
  420.7 66.6 reduce-scatter.14
  490.0 98.0 reduce-scatter.10
  590.4 31.9 all-reduce.3
  625.8 71.7 reduce-scatter.16
  701.6 75.1 reduce-scatter.12
where the time goes:
time: 787 us; the launch traced here: 786 us
  waiting for transfers between devices  561 us (71%)
  blocking collectives  112 us (14%)
  matrix products  51.6 us (7%)
  other arithmetic  35.4 us (4%)
  between operations  16.8 us (2%)
  local copies, waits for them, and re-layouts  9.02 us (1%)
    all_gather x1, waiting for transfers between devices, shards(): lax.all_gather(column_w1[0], 'proto', axis=1, tiled=True)  99.9 us
    reduce_scatter x1, waiting for transfers between devices, shards(): lax.psum_scatter(contract_rows(row_block, grad_pre), 'dp', scatter_dimens...  88.1 us
    reduce_scatter x1, waiting for transfers between devices, shards(): lax.psum_scatter(partial_w1, 'proto', scatter_dimension=1, tiled=True)  79.2 us
    reduce_scatter x1, waiting for transfers between devices, shards(): lax.psum_scatter(projected, 'dp', scatter_dimension=0, tiled=True)  75.1 us
    reduce_scatter x1, waiting for transfers between devices, shards(): lax.psum_scatter(lax.dot_general(row_block, proto_s_b, (((1,), (1,)), (()...  60 us
    reduce_scatter x1, waiting for transfers between devices, shards(): lax.psum_scatter(contract_rows(row_block, grad_z), 'proto', scatter_dimen...  50.8 us
    reduce_scatter x1, waiting for transfers between devices, shards(): lax.psum_scatter(jnp.dot(row_block, teacher_w2, preferred_element_type=jn...  38.4 us
    all_gather x1, waiting for transfers between devices, shards(): full_w2 = lax.all_gather(student_w2, 'proto', axis=0, tiled=True)  35.9 us
  transfers between devices with their start and end apart: 10, of which 9 were waited for; matrix products, arithmetic and copies ran while one was open for 6% of the time, Pallas kernels for 0%

commit v1 on v0

v1 whole, which is shorter than its diff:
```python
import functools
import math

import jax
import jax.numpy as jnp
from jax import lax
from jax.experimental import pallas as pl
from jax.experimental.pallas import tpu as pltpu
from jax.sharding import PartitionSpec as P

epsilon = 1e-06
teacher_temp = 0.07
student_temp = 0.1
loss_scale = 1048576.0


def select_rows(cls_tokens, patches, mask_index):
    picked = jax.vmap(lambda patch_set, index_set: patch_set[index_set])(patches, mask_index)
    joined = jnp.concatenate([cls_tokens[:, None, :], picked], axis=1)
    return joined.reshape(-1, cls_tokens.shape[-1])


def normalize_rows(bottle):
    inverse = lax.rsqrt(jnp.sum(bottle * bottle, axis=-1, keepdims=True) + epsilon)
    return (bottle * inverse, inverse)


def normalize_columns(proto):
    inverse = lax.rsqrt(jnp.sum(proto * proto, axis=0, keepdims=True) + epsilon)
    return (proto * inverse, inverse)


def gelu_grad(preact):
    normal_cdf = 0.5 * (1.0 + lax.erf(preact * 0.7071067811865476))
    normal_pdf = jnp.exp(-0.5 * preact * preact) * 0.3989422804014327
    return normal_cdf + preact * normal_pdf


def contract_rows(left, right):
    return lax.dot_general(
        left, right, (((0,), (0,)), ((), ())), preferred_element_type=jnp.float32
    )


def exchange_kernel(jobs, *refs):
    count = len(jobs)
    sources, results = refs[:count], refs[count : 2 * count]
    sends, arrivals, keep = refs[2 * count :]
    axes = sorted({axis for axis, _ in jobs})
    barrier = pltpu.get_barrier_semaphore()
    greeted = 0
    for axis in axes:
        ways = lax.axis_size(axis)
        me = lax.axis_index(axis)
        for step in range(1, ways):
            pl.semaphore_signal(
                barrier,
                inc=1,
                device_id={axis: lax.rem(me + step, ways)},
                device_id_type=pl.DeviceIdType.MESH,
            )
        greeted += ways - 1
    pl.semaphore_wait(barrier, greeted)
    most = max(lax.axis_size(axis) for axis in axes)
    pending = []
    for step in range(1, most):
        for job, (axis, gather) in enumerate(jobs):
            ways = lax.axis_size(axis)
            if step >= ways:
                continue
            me = lax.axis_index(axis)
            peer = lax.rem(me + step, ways)
            copy = pltpu.make_async_remote_copy(
                src_ref=sources[job] if gather else sources[job].at[peer],
                dst_ref=results[job].at[me],
                send_sem=sends.at[job, step],
                recv_sem=arrivals.at[job, step],
                device_id={axis: peer},
                device_id_type=pl.DeviceIdType.MESH,
            )
            copy.start()
            pending.append(copy)
    for job, (axis, gather) in enumerate(jobs):
        me = lax.axis_index(axis)
        copy = pltpu.make_async_copy(
            sources[job] if gather else sources[job].at[me], results[job].at[me], keep.at[job]
        )
        copy.start()
        pending.append(copy)
    for copy in pending:
        copy.wait()


def exchange(collective_id, *jobs):
    shapes, sent = [], 0
    for array, axis, gather in jobs:
        block = array.shape if gather else array.shape[1:]
        ways = lax.axis_size(axis)
        shapes.append(jax.ShapeDtypeStruct((ways,) + block, array.dtype))
        sent += ways * array.dtype.itemsize * math.prod(block)
    most = max(lax.axis_size(axis) for _, axis, _ in jobs)
    count = len(jobs)
    return pl.pallas_call(
        functools.partial(exchange_kernel, tuple((axis, gather) for _, axis, gather in jobs)),
        out_shape=shapes,
        in_specs=[pl.BlockSpec(memory_space=pl.ANY)] * count,
        out_specs=[pl.BlockSpec(memory_space=pl.ANY)] * count,
        scratch_shapes=[
            pltpu.SemaphoreType.DMA((count, most)),
            pltpu.SemaphoreType.DMA((count, most)),
            pltpu.SemaphoreType.DMA((count,)),
        ],
        compiler_params=pltpu.CompilerParams(collective_id=collective_id, has_side_effects=True),
        cost_estimate=pl.CostEstimate(flops=0, bytes_accessed=2 * sent, transcendentals=0),
    )(*[array for array, _, _ in jobs])


def shards(
    student_cls,
    student_patches,
    teacher_cls,
    teacher_patches,
    mask_index,
    crop_pair,
    center,
    student_w1,
    student_w2,
    teacher_w1,
    teacher_w2,
    student_proto,
    teacher_proto,
):
    row_span = mask_index.shape[1] + 1
    masked_count = mask_index.shape[1]
    local_crops = student_cls.shape[0]
    proto_ways = lax.axis_size("proto")
    data_ways = lax.axis_size("dp")
    data_index = lax.axis_index("dp")
    crop_group = local_crops * proto_ways
    own_rows = local_crops * row_span
    group_rows = crop_group * row_span
    all_rows = group_rows * data_ways
    crops_total = crop_group * data_ways
    width = student_cls.shape[1]
    bottleneck = student_w2.shape[1]
    hidden_block = student_w1.shape[1]
    share = student_proto.shape[1] // data_ways

    rows_student = select_rows(student_cls, student_patches, mask_index)
    rows_teacher = select_rows(teacher_cls, teacher_patches, mask_index)
    pair_tile = jnp.broadcast_to(crop_pair[:, None, None], (local_crops, 8, 128))
    student_all, teacher_all, pairs, first_s, first_t = exchange(
        0,
        (rows_student, "proto", True),
        (rows_teacher, "proto", True),
        (pair_tile, "proto", True),
        (student_w1, "dp", True),
        (teacher_w1, "dp", True),
    )
    student_all = student_all.reshape(group_rows, width)
    teacher_all = teacher_all.reshape(group_rows, width)
    pairs = pairs[:, :, 0, 0].reshape(crop_group)

    preact = jnp.dot(
        student_all, first_s.reshape(width, hidden_block), preferred_element_type=jnp.float32
    )
    hidden = jax.nn.gelu(preact, approximate=False).astype(jnp.bfloat16)
    part_s = jnp.dot(hidden, student_w2, preferred_element_type=jnp.float32)
    teacher_pre = jnp.dot(
        teacher_all, first_t.reshape(width, hidden_block), preferred_element_type=jnp.float32
    )
    teacher_hidden = jax.nn.gelu(teacher_pre, approximate=False).astype(jnp.bfloat16)
    part_t = jnp.dot(teacher_hidden, teacher_w2, preferred_element_type=jnp.float32)
    by_crop = part_t.reshape(crop_group, row_span, bottleneck)
    by_crop = jnp.concatenate([by_crop[:, 0][pairs][:, None], by_crop[:, 1:]], axis=1)
    parts = jnp.concatenate([part_s, by_crop.reshape(group_rows, bottleneck)], axis=1)
    (parts,) = exchange(1, (parts.reshape(proto_ways, own_rows, 2 * bottleneck), "proto", False))
    bottles = jnp.sum(parts, axis=0)
    unit_s, inverse_s = normalize_rows(bottles[:, :bottleneck])
    unit_t, _ = normalize_rows(bottles[:, bottleneck:])
    packed = jnp.concatenate([unit_s, unit_t], axis=1).astype(jnp.bfloat16)
    (group_units,) = exchange(2, (packed, "proto", True))
    (all_units,) = exchange(3, (group_units.reshape(group_rows, 2 * bottleneck), "dp", True))
    all_units = all_units.reshape(all_rows, 2 * bottleneck)
    rows_s = all_units[:, :bottleneck]
    rows_t = all_units[:, bottleneck:]

    own_s = lax.dynamic_slice_in_dim(student_proto, data_index * share, share, axis=1)
    own_t = lax.dynamic_slice_in_dim(teacher_proto, data_index * share, share, axis=1)
    own_center = lax.dynamic_slice_in_dim(center, data_index * share, share, axis=1)
    proto_unit, col_inverse = normalize_columns(own_s)
    teacher_unit, _ = normalize_columns(own_t)
    proto_s_b = proto_unit.astype(jnp.bfloat16)
    proto_t_b = teacher_unit.astype(jnp.bfloat16)
    is_cls = jnp.arange(all_rows, dtype=jnp.int32) % row_span == 0
    shift = jnp.where(is_cls[:, None], own_center[0][None, :], own_center[1][None, :])
    logit_s = jnp.dot(rows_s, proto_s_b, preferred_element_type=jnp.float32) / student_temp
    logit_t = (
        jnp.dot(rows_t, proto_t_b, preferred_element_type=jnp.float32) - shift
    ) / teacher_temp
    exp_s = jnp.exp(logit_s)
    exp_t = jnp.exp(logit_t)
    sums = jnp.stack(
        [jnp.sum(exp_t, axis=1), jnp.sum(exp_s, axis=1), jnp.sum(exp_t * logit_s, axis=1)]
    )
    (sums,) = exchange(4, (sums.reshape(-1, 128), "proto", True))
    (sums,) = exchange(5, (jnp.sum(sums, axis=0), "dp", True))
    total_t, total_s, cross = jnp.sum(sums, axis=0).reshape(3, all_rows)
    weights = jnp.where(is_cls, 1.0 / crops_total, 1.0 / (crops_total * masked_count)).astype(
        jnp.float32
    )
    weighted_loss = weights * (jnp.log(total_s) - cross / total_t)
    loss_value = (
        jnp.sum(lax.dynamic_slice_in_dim(weighted_loss, data_index * group_rows, group_rows))
        * data_ways
    ).reshape(1)
    factor = loss_scale / student_temp * weights
    dscore = (
        exp_s * (factor / total_s)[:, None] - exp_t * (factor / total_t)[:, None]
    ).astype(jnp.bfloat16)
    grad_units = lax.dot_general(
        dscore, proto_s_b, (((1,), (1,)), ((), ())), preferred_element_type=jnp.float32
    )
    grad_cols = contract_rows(rows_s, dscore)
    projected = col_inverse * (
        grad_cols - proto_unit * jnp.sum(proto_unit * grad_cols, axis=0, keepdims=True)
    )
    (grad_units,) = exchange(
        6, (grad_units.reshape(data_ways, group_rows, bottleneck), "dp", False)
    )
    grad_units = jnp.sum(grad_units, axis=0).reshape(proto_ways, own_rows, bottleneck)
    projected = projected.astype(jnp.bfloat16).reshape(
        data_ways, bottleneck // data_ways, share
    )
    grad_units, projected = exchange(
        7, (grad_units, "proto", False), (projected, "dp", False)
    )
    grad_proto = (
        projected.transpose(1, 0, 2)
        .reshape(bottleneck // data_ways, data_ways * share)
        .astype(jnp.float32)
    )
    grad_units = jnp.sum(grad_units, axis=0)
    grad_z = (
        inverse_s * (grad_units - unit_s * jnp.sum(unit_s * grad_units, axis=1, keepdims=True))
    ).astype(jnp.bfloat16)
    (grad_z,) = exchange(8, (grad_z, "proto", True))
    grad_z = grad_z.reshape(group_rows, bottleneck)

    grad_hidden = lax.dot_general(
        grad_z, student_w2, (((1,), (1,)), ((), ())), preferred_element_type=jnp.float32
    )
    grad_pre = (grad_hidden * gelu_grad(preact)).astype(jnp.bfloat16)
    part_w1 = contract_rows(student_all, grad_pre).astype(jnp.bfloat16)
    part_w2 = contract_rows(hidden, grad_z).astype(jnp.bfloat16)
    part_w1, part_w2 = exchange(
        9,
        (part_w1.reshape(data_ways, width // data_ways, hidden_block), "dp", False),
        (part_w2, "dp", True),
    )
    grad_w1 = jnp.sum(part_w1.astype(jnp.float32), axis=0)
    grad_w2 = jnp.sum(part_w2.astype(jnp.float32), axis=0)
    return (loss_value, grad_w1, grad_w2, grad_proto)


def solution(mesh):
    placed = (
        P(("dp", "proto"), None),
        P(("dp", "proto"), None, None),
        P(("dp", "proto"), None),
        P(("dp", "proto"), None, None),
        P(("dp", "proto"), None),
        P(("dp", "proto")),
        P(None, "proto"),
        P("dp", "proto"),
        P("proto", None),
        P("dp", "proto"),
        P("proto", None),
        P(None, "proto"),
        P(None, "proto"),
    )
    return jax.shard_map(
        shards,
        mesh=mesh,
        in_specs=placed,
        out_specs=(P("dp"), P("dp", "proto"), P("proto", None), P("dp", "proto")),
        check_vma=False,
    )
```

time: 787 us -> 217 us (0.28)
  waiting for transfers between devices: 561 us -> 0 us
  Pallas kernels: 0 us -> 145 us
  blocking collectives: 112 us -> 0 us
  matrix products: 51.6 us -> 29 us
  between operations: 16.8 us -> 3.46 us
    reduce_scatter x6 -> x0, waiting for transfers between devices: 392 us -> none  [the longest x1 88.1 us: shards(): lax.psum_scatter(contract_rows(row_block, grad_pre), 'dp', scatter_dimens...]
    pallas_call x0 -> x10, Pallas kernels: none -> 145 us  [exchange(): pl.pallas_call(functools.partial(exchange_kernel, tuple(((axis, gather) f...]
    all_gather x3 -> x0, waiting for transfers between devices: 136 us -> none  [the longest x1 99.9 us: shards(): lax.all_gather(column_w1[0], 'proto', axis=1, tiled=True)]
    all_gather x2 -> x0, blocking collectives: 64.6 us -> none  [the longest x1 33.9 us: shards(): teacher_all = lax.all_gather(rows_teacher, 'proto', axis=0, tiled=True)]
    psum x2 -> x0, blocking collectives: 36.5 us -> none  [the longest x1 19.2 us: shards(): lax.psum((jnp.sum(jnp.exp(logit_t), axis=1), jnp.sum(jnp.exp(logit_s), ax...]
    psum x1 -> x0, waiting for transfers between devices: 33.1 us -> none  [shards(): grad_w2 = lax.psum(partial_w2, 'dp')]
    mul x3 -> x0, other arithmetic: 12.4 us -> none  [the longest x1 12.4 us: shards(): col_inverse * (grad_cols - proto_unit * jnp.sum(proto_unit * grad_cols, a...]
    dot_general x6, matrix products: 33.7 us -> 21.8 us  [the longest x1 9.94 us: shards(): jnp.dot(rows_t, proto_t_b, preferred_element_type=jnp.float32) - shift]
  transfers between devices with their start and end apart: 10 -> 0, of which waited for: 9 -> 0; matrix products, arithmetic and copies ran while one was open for 6% -> 0% of each run, Pallas kernels for 0% -> 0%
where the time goes in v1:
time: 217 us; the launch traced here: 215 us
  Pallas kernels  145 us (67%)
  other arithmetic  30.4 us (14%)
  matrix products  29 us (13%)
  local copies, waits for them, and re-layouts  7.77 us (4%)
  between operations  3.46 us (2%)
    pallas_call x10, Pallas kernels, exchange(): pl.pallas_call(functools.partial(exchange_kernel, tuple(((axis, gather) f...  145 us
    dot_general x1, matrix products, shards(): jnp.dot(rows_t, proto_t_b, preferred_element_type=jnp.float32) - shift  9.94 us
    convert_element_type x1, other arithmetic, shards(): dscore = (exp_s * (factor / total_s)[:, None] - exp_t * (factor / total_t...  7.61 us
    dot_general x3, matrix products, contract_rows(): lax.dot_general(left, right, (((0,), (0,)), ((), ())), preferred_element_...  7.19 us

profile of v1, /device:TPU:0, one launch (start us, length us, event | category | flops | bytes accessed | tf_op | source)
XLA Modules:
  0.0 215.4 jit_solution(17338647417643976358)
XLA Ops:
  3.6 2.6 %multiply_reduce_fusion.2 = (f32[2048]{0:T(1024)S(1)}, f32[2048]{0:T(1024)S(1)}) fusion(f32[256,8192]{1,0:T(8,128)} %param.24, s32[]{:T(128)S(6)} %select_n.68, f32[256,8192]{1,0:T(8,128)} %param.25), kind=kLoop, calls=%fused_computation.12 | loop fusion | flops 2093056 | bytes 4210692 | tf_op jit(solution)/shard_map/reduce_sum | solution.py:29
  10.3 32.9 %shard_map.156 = (bf16[8,32,1536]{2,1,0:T(8,128)(2,1)}, bf16[8,32,1536]{2,1,0:T(8,128)(2,1)}, s32[8,1,8,128]{3,2,1,0:T(8,128)}, bf16[4,384,256]{2,1,0:T(8,128)(2,1)}, bf16[4,384,256]{2,1,0:T(8,128)(2,1)}) custom-call(bf16[32,1536]{1,0:T(8,128)(2,1)} %get-tuple-element.41.refs_0_, bf16[32,1536]{1,0:T(8,128)(2,1)} %get-tuple-element.42.refs_1_, ...), custom_call_target="tpu_custom_call" | custom-call | bytes 6356992 | tf_op jit(solution)/shard_map/pallas_call | solution.py:103
  43.1 2.2 %fusion.15 = (bf16[256,256]{1,0:T(8,128)(2,1)S(1)}, f32[256,256]{1,0:T(8,128)S(1)}) fusion(bf16[256,1536]{1,0:T(8,128)(2,1)} %bitcast.106, bf16[1536,256]{1,0:T(8,128)(2,1)} %bitcast.110), kind=kOutput, calls=%fused_computation.36 | convolution fusion | flops 205586432 | bytes 1966080 | tf_op jit(solution)/shard_map/dot_general | solution.py:164
  46.6 2.4 %fusion.47 = f32[256,256]{1,0:T(8,128)S(1)} fusion(bf16[256,256]{1,0:T(8,128)(2,1)S(1)} %copy-done.5, bf16[256,1536]{1,0:T(8,128)(2,1)} %bitcast.108, bf16[1536,256]{1,0:T(8,128)(2,1)} %bitcast.109), kind=kOutput, calls=%fused_computation.83 | convolution fusion | flops 239140864 | bytes 1966080 | tf_op jit(solution)/shard_map/dot_general | solution.py:173
  50.6 21.3 %shard_map.157 = f32[8,32,512]{2,1,0:T(8,128)} custom-call(f32[8,32,512]{2,1,0:T(8,128)} %maximum_maximum_fusion.refs_0_), custom_call_target="tpu_custom_call" | custom-call | bytes 1048576 | tf_op jit(solution)/shard_map/pallas_call | solution.py:103
  73.8 11.2 %shard_map.158 = bf16[8,32,512]{2,1,0:T(8,128)(2,1)} custom-call(bf16[32,512]{1,0:T(8,128)(2,1)} %pad_maximum_fusion.refs_0_), custom_call_target="tpu_custom_call" | custom-call | bytes 524288 | tf_op jit(solution)/shard_map/pallas_call | solution.py:103
  84.9 13.7 %shard_map.159 = bf16[4,256,512]{2,1,0:T(8,128)(2,1)} custom-call(bf16[256,512]{1,0:T(8,128)(2,1)} %bitcast.86), custom_call_target="tpu_custom_call" | custom-call | bytes 2097152 | tf_op jit(solution)/shard_map/pallas_call | solution.py:103
  98.7 3.1 %fusion.8 = f32[1024,2048]{1,0:T(8,128)S(1)} fusion(bf16[1024,512]{1,0:T(8,128)(2,1)} %bitcast.80, f32[256,8192]{1,0:T(8,128)} %param.24, s32[]{:T(128)S(6)} %select_n.68, f32[2048]{0:T(1024)S(1)} %add_rsqrt_fusion), kind=kOutput, calls=%fused_computation.28 | convolution fusion | flops 1074790400 | bytes 11018244 | tf_op jit(solution)/shard_map/dot_general | solution.py:197
  101.8 9.9 %fusion = (f32[1024]{0:T(1024)S(1)}, f32[1024]{0:T(1024)S(1)}, f32[1024]{0:T(1024)S(1)}, f32[1024,2048]{1,0:T(8,128)}) fusion(f32[2048]{0:T(1024)S(1)} %bitcast.99, f32[2048]{0:T(1024)S(1)} %bitcast.97, pred[1024]{0:T(1024)(128)(4,1)S(1)} %fusion.52, f32[1024,2048]{1,0:T(8,128)S(1)} %fusion.8, f32[256,8192]{1,0:T(8,128)} %param.25, s32[]{:T(128)S(6)} %select_n.68, ...), kind=kOutput, calls=%fused_computation.7 | convolution fusion | flops 1091564544 | bytes 19436548 | tf_op jit(solution)/shard_map/dot_general | solution.py:199
  112.4 8.4 %shard_map.160 = f32[8,24,128]{2,1,0:T(8,128)} custom-call(f32[24,128]{1,0:T(8,128)} %reshape.163.refs_0_), custom_call_target="tpu_custom_call" | custom-call | bytes 196608 | tf_op jit(solution)/shard_map/pallas_call | solution.py:103
  122.3 4.1 %shard_map.161 = f32[4,24,128]{2,1,0:T(8,128)} custom-call(f32[24,128]{1,0:T(8,128)} %reduce_sum.161.refs_0_), custom_call_target="tpu_custom_call" | custom-call | bytes 98304 | tf_op jit(solution)/shard_map/pallas_call | solution.py:103
  128.5 7.6 %subtract_convert_fusion = bf16[1024,2048]{1,0:T(8,128)(2,1)S(1)} fusion(f32[1024,2048]{1,0:T(8,128)} %copy-done.1, f32[1024,2048]{1,0:T(8,128)} %get-tuple-element.36, f32[1024]{0:T(1024)S(1)} %get-tuple-element.32, f32[1024]{0:T(1024)S(1)} %get-tuple-element.31, f32[2048]{0:T(1024)S(1)} %bitcast.100, f32[2048]{0:T(1024)S(1)} %bitcast.98, ...), kind=kLoop, calls=%fused_computation.3 | loop fusion | flops 16777216 | bytes 20997120 | tf_op jit(solution)/shard_map/convert_element_type | solution.py:220
  136.1 3.9 %fusion.10 = f32[1024,256]{1,0:T(8,128)} fusion(bf16[1024,2048]{1,0:T(8,128)(2,1)S(1)} %subtract_convert_fusion, f32[256,8192]{1,0:T(8,128)} %param.24, s32[]{:T(128)S(6)} %select_n.68, f32[2048]{0:T(1024)S(1)} %add_rsqrt_fusion), kind=kOutput, calls=%fused_computation.33 | convolution fusion | flops 1074790400 | bytes 7348228 | tf_op jit(solution)/shard_map/dot_general | solution.py:221
  140.0 3.0 %multiply_reduce_fusion.1 = (f32[2048]{0:T(1024)S(1)}, f32[256,2048]{1,0:T(8,128)S(1)}) fusion(f32[256,8192]{1,0:T(8,128)} %param.24, s32[]{:T(128)S(6)} %select_n.68, f32[2048]{0:T(1024)S(1)} %add_rsqrt_fusion, bf16[1024,2048]{1,0:T(8,128)(2,1)S(1)} %subtract_convert_fusion, bf16[1024,512]{1,0:T(8,128)(2,1)S(1)} %bitcast.82), kind=kOutput, calls=%fused_computation.11 | convolution fusion | flops 1075312640 | bytes 8929284 | tf_op jit(solution)/shard_map/dot_general | solution.py:40
  143.0 3.1 %multiply_convert_fusion = bf16[256,2048]{1,0:T(8,128)(2,1)} fusion(f32[256,2048]{1,0:T(8,128)S(1)} %get-tuple-element.38, f32[256,8192]{1,0:T(8,128)} %param.24, s32[]{:T(128)S(6)} %select_n.68, f32[2048]{0:T(1024)S(1)} %get-tuple-element.37, f32[2048]{0:T(1024)S(1)} %add_rsqrt_fusion), kind=kLoop, calls=%fused_computation.10 | loop fusion | flops 2621440 | bytes 5259268 | tf_op jit(solution)/shard_map/convert_element_type | solution.py:232
  146.1 12.5 %shard_map.162 = f32[4,256,256]{2,1,0:T(8,128)} custom-call(f32[4,256,256]{2,1,0:T(8,128)} %bitcast.87), custom_call_target="tpu_custom_call" | custom-call | bytes 2097152 | tf_op jit(solution)/shard_map/pallas_call | solution.py:103
  158.6 2.0 reduce_sum.164
  160.7 16.2 %shard_map.163 = (f32[8,32,256]{2,1,0:T(8,128)}, bf16[4,64,2048]{2,1,0:T(8,128)(2,1)}) custom-call(f32[8,32,256]{2,1,0:T(8,128)} %bitcast.85, bf16[4,64,2048]{2,1,0:T(8,128)(2,1)} %bitcast.83), custom_call_target="tpu_custom_call" | custom-call | bytes 2621440 | tf_op jit(solution)/shard_map/pallas_call | solution.py:103
  178.7 7.0 %shard_map.164 = bf16[8,32,256]{2,1,0:T(8,128)(2,1)} custom-call(bf16[32,256]{1,0:T(8,128)(2,1)} %multiply_convert_fusion.3.refs_0_), custom_call_target="tpu_custom_call" | custom-call | bytes 262144 | tf_op jit(solution)/shard_map/pallas_call | solution.py:103
  185.7 2.4 %convolution_convert_fusion = bf16[1536,256]{1,0:T(8,128)(2,1)} fusion(bf16[256,1536]{1,0:T(8,128)(2,1)S(1)} %bitcast.107, bf16[256,256]{1,0:T(8,128)(2,1)} %bitcast.91, bf16[256,256]{1,0:T(8,128)(2,1)S(1)} %copy-done.3, f32[256,256]{1,0:T(8,128)S(1)} %get-tuple-element.35), kind=kOutput, calls=%fused_computation.8 | convolution fusion | flops 235929600 | bytes 2097152 | tf_op jit(solution)/shard_map/dot_general | solution.py:40
  188.2 1.8 convolution_convert_fusion.1.refs_1_
  190.0 17.5 %shard_map.165 = (bf16[4,384,256]{2,1,0:T(8,128)(2,1)}, bf16[4,256,256]{2,1,0:T(8,128)(2,1)}) custom-call(bf16[4,384,256]{2,1,0:T(8,128)(2,1)} %bitcast.89, bf16[256,256]{1,0:T(8,128)(2,1)} %convolution_convert_fusion.1.refs_1_), custom_call_target="tpu_custom_call" | custom-call | bytes 2621440 | tf_op jit(solution)/shard_map/pallas_call | solution.py:103
  207.5 2.0 convert_reduce_fusion
  209.5 1.8 convert_reduce_fusion.1
  (50 shorter events, 19.2 us)
Async XLA Ops:
  0.6 5.6 %copy-start = (bf16[1,256,1536]{2,1,0:T(8,128)(2,1)S(1)}, bf16[1,256,1536]{2,1,0:T(8,128)(2,1)}, u32[]{:S(2)}) copy-start(bf16[1,256,1536]{2,1,0:T(8,128)(2,1)} %param.16) | copy-start | bytes 2359300
  0.6 45.8 %copy-start.3 = (bf16[256,256]{1,0:T(8,128)(2,1)S(1)}, bf16[256,256]{1,0:T(8,128)(2,1)}, u32[]{:S(2)}) copy-start(bf16[256,256]{1,0:T(8,128)(2,1)} %param.21) | copy-start | bytes 393220
  0.7 46.0 %copy-start.5 = (bf16[256,256]{1,0:T(8,128)(2,1)S(1)}, bf16[256,256]{1,0:T(8,128)(2,1)}, u32[]{:S(2)}) copy-start(bf16[256,256]{1,0:T(8,128)(2,1)} %param.23) | copy-start | bytes 393220
  98.7 3.1 %copy-start.2 = (bf16[4,256,512]{2,1,0:T(8,128)(2,1)S(1)}, bf16[4,256,512]{2,1,0:T(8,128)(2,1)}, u32[]{:S(2)}) copy-start(bf16[4,256,512]{2,1,0:T(8,128)(2,1)} %shard_map.159) | copy-start | bytes 3145732
  101.8 10.0 %copy-start.1 = (f32[1024,2048]{1,0:T(8,128)}, f32[1024,2048]{1,0:T(8,128)S(1)}, u32[]{:S(2)}) copy-start(f32[1024,2048]{1,0:T(8,128)S(1)} %fusion.8) | copy-start | bytes 25165828
  140.0 45.7 %copy-start.4 = (bf16[8,32,1536]{2,1,0:T(8,128)(2,1)S(1)}, bf16[8,32,1536]{2,1,0:T(8,128)(2,1)}, u32[]{:S(2)}) copy-start(bf16[8,32,1536]{2,1,0:T(8,128)(2,1)} %get-tuple-element.13) | copy-start | bytes 2359300

commit v2 on v1

--- a/solution.py
+++ b/solution.py
@@ -12,6 +12,8 @@
 teacher_temp = 0.07
 student_temp = 0.1
 loss_scale = 1048576.0
+PROTO = ("proto",)
+DATA = ("dp",)
 
 
 def select_rows(cls_tokens, patches, mask_index):
@@ -42,66 +44,181 @@
     )
 
 
+def place(rel):
+    spot = {}
+    for axis, (far, near) in rel.items():
+        high, low = split_axis(axis)
+        me = lax.axis_index(axis)
+        spot[axis] = lax.rem(me // low + far, high) * low + lax.rem(me % low + near, low)
+    return spot
+
+
+def split_axis(axis):
+    ways = lax.axis_size(axis)
+    return (ways // 2, 2) if ways % 2 == 0 else (ways, 1)
+
+
+def offsets(axes):
+    found = [{axis: (0, 0) for axis in axes}]
+    for axis in axes:
+        high, low = split_axis(axis)
+        found = [
+            {**rel, axis: (far, near)}
+            for far in range(high)
+            for near in range(low)
+            for rel in found
+        ]
+    return found
+
+
+def key(rel):
+    return tuple(sorted((axis, step) for axis, step in rel.items() if step != (0, 0)))
+
+
+def steps_of(axes):
+    return [
+        (axis, part, split_axis(axis)[part])
+        for axis in axes
+        for part in (0, 1)
+        if split_axis(axis)[part] > 1
+    ]
+
+
+def moved(rel, axis, part, offset):
+    step = list(rel[axis])
+    step[part] = offset
+    return {**rel, axis: tuple(step)}
+
+
+def slot(spot, axes):
+    index = 0
+    for axis in sorted(axes):
+        index = index * lax.axis_size(axis) + spot[axis]
+    return index
+
+
 def exchange_kernel(jobs, *refs):
     count = len(jobs)
     sources, results = refs[:count], refs[count : 2 * count]
     sends, arrivals, keep = refs[2 * count :]
-    axes = sorted({axis for axis, _ in jobs})
+    peers = {}
+    for axes, gather in jobs:
+        if gather:
+            own = {axis: (0, 0) for axis in axes}
+            reached = [
+                moved(own, axis, part, offset)
+                for axis, part, size in steps_of(axes)
+                for offset in range(1, size)
+            ]
+        else:
+            reached = offsets(axes)[1:]
+        for rel in reached:
+            peers[key(rel)] = {axis: step for axis, step in rel.items() if step != (0, 0)}
     barrier = pltpu.get_barrier_semaphore()
-    greeted = 0
-    for axis in axes:
-        ways = lax.axis_size(axis)
-        me = lax.axis_index(axis)
-        for step in range(1, ways):
-            pl.semaphore_signal(
-                barrier,
-                inc=1,
-                device_id={axis: lax.rem(me + step, ways)},
-                device_id_type=pl.DeviceIdType.MESH,
-            )
-        greeted += ways - 1
-    pl.semaphore_wait(barrier, greeted)
-    most = max(lax.axis_size(axis) for axis in axes)
-    pending = []
-    for step in range(1, most):
-        for job, (axis, gather) in enumerate(jobs):
-            ways = lax.axis_size(axis)
-            if step >= ways:
-                continue
-            me = lax.axis_index(axis)
-            peer = lax.rem(me + step, ways)
-            copy = pltpu.make_async_remote_copy(
-                src_ref=sources[job] if gather else sources[job].at[peer],
-                dst_ref=results[job].at[me],
-                send_sem=sends.at[job, step],
-                recv_sem=arrivals.at[job, step],
-                device_id={axis: peer},
-                device_id_type=pl.DeviceIdType.MESH,
-            )
-            copy.start()
-            pending.append(copy)
-    for job, (axis, gather) in enumerate(jobs):
-        me = lax.axis_index(axis)
-        copy = pltpu.make_async_copy(
-            sources[job] if gather else sources[job].at[me], results[job].at[me], keep.at[job]
+    for rel in peers.values():
+        pl.semaphore_signal(
+            barrier, inc=1, device_id=place(rel), device_id_type=pl.DeviceIdType.MESH
+        )
+    pl.semaphore_wait(barrier, len(peers))
+
+    sent = []
+    held = [[{axis: (0, 0) for axis in axes}] for axes, _ in jobs]
+    numbers = [{key(rel): n for n, rel in enumerate(offsets(axes))} for axes, _ in jobs]
+    arriving = [{} for _ in jobs]
+
+    def send(job, source, owner, to, number):
+        copy = pltpu.make_async_remote_copy(
+            src_ref=source,
+            dst_ref=results[job].at[slot(owner, jobs[job][0])],
+            send_sem=sends.at[job, number],
+            recv_sem=arrivals.at[job, number],
+            device_id=to,
+            device_id_type=pl.DeviceIdType.MESH,
         )
         copy.start()
-        pending.append(copy)
-    for copy in pending:
+        sent.append(copy)
+
+    def pass_on(job, rel, step):
+        axis, part, size = step
+        axes = jobs[job][0]
+        if key(rel) in arriving[job]:
+            arriving[job].pop(key(rel)).wait_recv()
+        owner = place(rel)
+        source = results[job].at[slot(owner, axes)] if key(rel) else sources[job]
+        for offset in range(1, size):
+            landed = moved(rel, axis, part, size - offset)
+            to = place({axis: hop(part, offset)})
+            send(job, source, owner, to, numbers[job][key(landed)])
+            arriving[job][key(landed)] = copy_in(job, landed)
+
+    def hop(part, offset):
+        return (offset, 0) if part == 0 else (0, offset)
+
+    def copy_in(job, landed):
+        here = results[job].at[slot(place(landed), jobs[job][0])]
+        number = numbers[job][key(landed)]
+        return pltpu.make_async_remote_copy(
+            src_ref=here,
+            dst_ref=here,
+            send_sem=sends.at[job, number],
+            recv_sem=arrivals.at[job, number],
+            device_id=place({axis: (0, 0) for axis in jobs[job][0]}),
+            device_id_type=pl.DeviceIdType.MESH,
+        )
+
+    phases = [steps_of(axes) if gather else [] for axes, gather in jobs]
+    local = []
+    for phase in range(max([1] + [len(steps) for steps in phases])):
+        before = [list(rels) for rels in held]
+        for turn in range(max(len(rels) for rels in before)):
+            for job, (axes, gather) in enumerate(jobs):
+                if not gather or phase >= len(phases[job]) or turn >= len(before[job]):
+                    continue
+                axis, part, size = phases[job][phase]
+                rel = before[job][turn]
+                pass_on(job, rel, phases[job][phase])
+                held[job] += [moved(rel, axis, part, size - offset) for offset in range(1, size)]
+        if phase == 0:
+            for job, (axes, gather) in enumerate(jobs):
+                if not gather:
+                    me = place({axis: (0, 0) for axis in axes})
+                    for rel in offsets(axes)[1:]:
+                        to = place(rel)
+                        (axis,) = axes
+                        high, low = split_axis(axis)
+                        back = {axis: ((high - rel[axis][0]) % high, (low - rel[axis][1]) % low)}
+                        number = numbers[job][key(back)]
+                        send(job, sources[job].at[slot(to, axes)], me, to, number)
+                        arriving[job][key(back)] = copy_in(job, back)
+            for job, (axes, gather) in enumerate(jobs):
+                me = slot(place({axis: (0, 0) for axis in axes}), axes)
+                copy = pltpu.make_async_copy(
+                    sources[job] if gather else sources[job].at[me],
+                    results[job].at[me],
+                    keep.at[job],
+                )
+                copy.start()
+                local.append(copy)
+    for waits in arriving:
+        for copy in waits.values():
+            copy.wait_recv()
+    for copy in sent:
+        copy.wait_send()
+    for copy in local:
         copy.wait()
 
 
 def exchange(collective_id, *jobs):
-    shapes, sent = [], 0
-    for array, axis, gather in jobs:
+    shapes, moved_bytes = [], 0
+    for array, axes, gather in jobs:
         block = array.shape if gather else array.shape[1:]
-        ways = lax.axis_size(axis)
+        ways = math.prod(lax.axis_size(axis) for axis in axes)
         shapes.append(jax.ShapeDtypeStruct((ways,) + block, array.dtype))
-        sent += ways * array.dtype.itemsize * math.prod(block)
-    most = max(lax.axis_size(axis) for _, axis, _ in jobs)
+        moved_bytes += ways * array.dtype.itemsize * math.prod(block)
+    most = max(shape.shape[0] for shape in shapes)
     count = len(jobs)
     return pl.pallas_call(
-        functools.partial(exchange_kernel, tuple((axis, gather) for _, axis, gather in jobs)),
+        functools.partial(exchange_kernel, tuple((axes, gather) for _, axes, gather in jobs)),
         out_shape=shapes,
         in_specs=[pl.BlockSpec(memory_space=pl.ANY)] * count,
         out_specs=[pl.BlockSpec(memory_space=pl.ANY)] * count,
@@ -111,7 +228,9 @@
             pltpu.SemaphoreType.DMA((count,)),
         ],
         compiler_params=pltpu.CompilerParams(collective_id=collective_id, has_side_effects=True),
-        cost_estimate=pl.CostEstimate(flops=0, bytes_accessed=2 * sent, transcendentals=0),
+        cost_estimate=pl.CostEstimate(
+            flops=0, bytes_accessed=2 * moved_bytes, transcendentals=0
+        ),
     )(*[array for array, _, _ in jobs])
 
 
@@ -151,11 +270,11 @@
     pair_tile = jnp.broadcast_to(crop_pair[:, None, None], (local_crops, 8, 128))
     student_all, teacher_all, pairs, first_s, first_t = exchange(
         0,
-        (rows_student, "proto", True),
-        (rows_teacher, "proto", True),
-        (pair_tile, "proto", True),
-        (student_w1, "dp", True),
-        (teacher_w1, "dp", True),
+        (rows_student, PROTO, True),
+        (rows_teacher, PROTO, True),
+        (pair_tile, PROTO, True),
+        (student_w1, DATA, True),
+        (teacher_w1, DATA, True),
     )
     student_all = student_all.reshape(group_rows, width)
     teacher_all = teacher_all.reshape(group_rows, width)
@@ -173,14 +292,19 @@
     part_t = jnp.dot(teacher_hidden, teacher_w2, preferred_element_type=jnp.float32)
     by_crop = part_t.reshape(crop_group, row_span, bottleneck)
     by_crop = jnp.concatenate([by_crop[:, 0][pairs][:, None], by_crop[:, 1:]], axis=1)
-    parts = jnp.concatenate([part_s, by_crop.reshape(group_rows, bottleneck)], axis=1)
-    (parts,) = exchange(1, (parts.reshape(proto_ways, own_rows, 2 * bottleneck), "proto", False))
-    bottles = jnp.sum(parts, axis=0)
-    unit_s, inverse_s = normalize_rows(bottles[:, :bottleneck])
-    unit_t, _ = normalize_rows(bottles[:, bottleneck:])
+    parts_s, parts_t = exchange(
+        1,
+        (part_s.reshape(proto_ways, own_rows, bottleneck), PROTO, False),
+        (
+            by_crop.astype(jnp.bfloat16).reshape(proto_ways, own_rows, bottleneck),
+            PROTO,
+            False,
+        ),
+    )
+    unit_s, inverse_s = normalize_rows(jnp.sum(parts_s, axis=0))
+    unit_t, _ = normalize_rows(jnp.sum(parts_t.astype(jnp.float32), axis=0))
     packed = jnp.concatenate([unit_s, unit_t], axis=1).astype(jnp.bfloat16)
-    (group_units,) = exchange(2, (packed, "proto", True))
-    (all_units,) = exchange(3, (group_units.reshape(group_rows, 2 * bottleneck), "dp", True))
+    (all_units,) = exchange(2, (packed, PROTO + DATA, True))
     all_units = all_units.reshape(all_rows, 2 * bottleneck)
     rows_s = all_units[:, :bottleneck]
     rows_t = all_units[:, bottleneck:]
@@ -203,8 +327,7 @@
     sums = jnp.stack(
         [jnp.sum(exp_t, axis=1), jnp.sum(exp_s, axis=1), jnp.sum(exp_t * logit_s, axis=1)]
     )
-    (sums,) = exchange(4, (sums.reshape(-1, 128), "proto", True))
-    (sums,) = exchange(5, (jnp.sum(sums, axis=0), "dp", True))
+    (sums,) = exchange(3, (sums.reshape(-1, 128), PROTO + DATA, True))
     total_t, total_s, cross = jnp.sum(sums, axis=0).reshape(3, all_rows)
     weights = jnp.where(is_cls, 1.0 / crops_total, 1.0 / (crops_total * masked_count)).astype(
         jnp.float32
@@ -226,25 +349,27 @@
         grad_cols - proto_unit * jnp.sum(proto_unit * grad_cols, axis=0, keepdims=True)
     )
     (grad_units,) = exchange(
-        6, (grad_units.reshape(data_ways, group_rows, bottleneck), "dp", False)
+        4, (grad_units.reshape(data_ways, group_rows, bottleneck), DATA, False)
     )
     grad_units = jnp.sum(grad_units, axis=0).reshape(proto_ways, own_rows, bottleneck)
     projected = projected.astype(jnp.bfloat16).reshape(
         data_ways, bottleneck // data_ways, share
     )
-    grad_units, projected = exchange(
-        7, (grad_units, "proto", False), (projected, "dp", False)
-    )
-    grad_proto = (
-        projected.transpose(1, 0, 2)
-        .reshape(bottleneck // data_ways, data_ways * share)
-        .astype(jnp.float32)
+    half = bottleneck // data_ways // 2
+    grad_units, upper = exchange(
+        5, (grad_units, PROTO, False), (projected[:, :half], DATA, False)
     )
     grad_units = jnp.sum(grad_units, axis=0)
     grad_z = (
         inverse_s * (grad_units - unit_s * jnp.sum(unit_s * grad_units, axis=1, keepdims=True))
     ).astype(jnp.bfloat16)
-    (grad_z,) = exchange(8, (grad_z, "proto", True))
+    grad_z, lower = exchange(6, (grad_z, PROTO, True), (projected[:, half:], DATA, False))
+    grad_proto = (
+        jnp.concatenate([upper, lower], axis=1)
+        .transpose(1, 0, 2)
+        .reshape(2 * half, data_ways * share)
+        .astype(jnp.float32)
+    )
     grad_z = grad_z.reshape(group_rows, bottleneck)
 
     grad_hidden = lax.dot_general(
@@ -254,9 +379,9 @@
     part_w1 = contract_rows(student_all, grad_pre).astype(jnp.bfloat16)
     part_w2 = contract_rows(hidden, grad_z).astype(jnp.bfloat16)
     part_w1, part_w2 = exchange(
-        9,
-        (part_w1.reshape(data_ways, width // data_ways, hidden_block), "dp", False),
-        (part_w2, "dp", True),
+        7,
+        (part_w1.reshape(data_ways, width // data_ways, hidden_block), DATA, False),
+        (part_w2, DATA, True),
     )
     grad_w1 = jnp.sum(part_w1.astype(jnp.float32), axis=0)
     grad_w2 = jnp.sum(part_w2.astype(jnp.float32), axis=0)

time: 217 us -> 196 us (0.903)
  Pallas kernels: 145 us -> 124 us
    pallas_call x10 -> x8, Pallas kernels: 145 us -> 124 us  [exchange(): pl.pallas_call(functools.partial(exchange_kernel, tuple(((axes, gather) f...]
where the time goes in v2:
time: 196 us; the launch traced here: 195 us
  Pallas kernels  124 us (63%)
  matrix products  29.6 us (15%)
  other arithmetic  29.1 us (15%)
  local copies, waits for them, and re-layouts  8.82 us (4%)
  between operations  3.44 us (2%)
    pallas_call x8, Pallas kernels, exchange(): pl.pallas_call(functools.partial(exchange_kernel, tuple(((axes, gather) f...  124 us
    dot_general x1, matrix products, shards(): jnp.dot(rows_t, proto_t_b, preferred_element_type=jnp.float32) - shift  9.96 us
    convert_element_type x1, other arithmetic, shards(): dscore = (exp_s * (factor / total_s)[:, None] - exp_t * (factor / total_t...  7.61 us
    dot_general x3, matrix products, contract_rows(): lax.dot_general(left, right, (((0,), (0,)), ((), ())), preferred_element_...  7.11 us

profile of v2, /device:TPU:0, one launch (start us, length us, event | category | flops | bytes accessed | tf_op | source)
XLA Modules:
  0.0 195.3 jit_solution(1725350498021946805)
XLA Ops:
  3.5 2.6 %multiply_reduce_fusion.2 = (f32[2048]{0:T(1024)S(1)}, f32[2048]{0:T(1024)S(1)}) fusion(f32[256,8192]{1,0:T(8,128)} %param.24, s32[]{:T(128)S(6)} %select_n.68, f32[256,8192]{1,0:T(8,128)} %param.25), kind=kLoop, calls=%fused_computation.12 | loop fusion | flops 2093056 | bytes 4210692 | tf_op jit(solution)/shard_map/reduce_sum | solution.py:31
  7.1 1.7 gather_fusion.1
  8.8 1.5 maximum_bitcast_fusion
  10.3 31.4 %shard_map.156 = (bf16[8,32,1536]{2,1,0:T(8,128)(2,1)}, bf16[8,32,1536]{2,1,0:T(8,128)(2,1)}, s32[8,1,8,128]{3,2,1,0:T(8,128)}, bf16[4,384,256]{2,1,0:T(8,128)(2,1)}, bf16[4,384,256]{2,1,0:T(8,128)(2,1)}) custom-call(bf16[32,1536]{1,0:T(8,128)(2,1)} %get-tuple-element.47.refs_0_, bf16[32,1536]{1,0:T(8,128)(2,1)} %get-tuple-element.48.refs_1_, ...), custom_call_target="tpu_custom_call" | custom-call | bytes 6356992 | tf_op jit(solution)/shard_map/pallas_call | solution.py:220
  41.7 2.2 %fusion.15 = (bf16[256,256]{1,0:T(8,128)(2,1)S(1)}, f32[256,256]{1,0:T(8,128)S(1)}) fusion(bf16[256,1536]{1,0:T(8,128)(2,1)} %bitcast.108, bf16[1536,256]{1,0:T(8,128)(2,1)} %bitcast.112), kind=kOutput, calls=%fused_computation.35 | convolution fusion | flops 205586432 | bytes 1966080 | tf_op jit(solution)/shard_map/dot_general | solution.py:283
  45.0 2.4 %fusion.47 = bf16[256,256]{1,0:T(8,128)(2,1)S(1)} fusion(bf16[256,256]{1,0:T(8,128)(2,1)S(1)} %copy-done.5, bf16[256,1536]{1,0:T(8,128)(2,1)} %bitcast.110, bf16[1536,256]{1,0:T(8,128)(2,1)} %bitcast.111), kind=kOutput, calls=%fused_computation.85 | convolution fusion | flops 239140864 | bytes 1835008 | tf_op jit(solution)/shard_map/dot_general | solution.py:292
  49.7 14.9 %shard_map.157 = (f32[8,32,256]{2,1,0:T(8,128)}, bf16[8,32,256]{2,1,0:T(8,128)(2,1)}) custom-call(f32[8,32,256]{2,1,0:T(8,128)} %bitcast.89, bf16[8,32,256]{2,1,0:T(8,128)(2,1)} %pad_maximum_fusion.refs_1_), custom_call_target="tpu_custom_call" | custom-call | bytes 786432 | tf_op jit(solution)/shard_map/pallas_call | solution.py:220
  67.5 15.4 %shard_map.158 = bf16[32,32,512]{2,1,0:T(8,128)(2,1)} custom-call(bf16[32,512]{1,0:T(8,128)(2,1)} %pad_maximum_fusion.1.refs_0_), custom_call_target="tpu_custom_call" | custom-call | bytes 2097152 | tf_op jit(solution)/shard_map/pallas_call | solution.py:220
  82.9 3.1 %fusion.8 = f32[1024,2048]{1,0:T(8,128)S(1)} fusion(bf16[1024,512]{1,0:T(8,128)(2,1)} %bitcast.82, f32[256,8192]{1,0:T(8,128)} %param.24, s32[]{:T(128)S(6)} %select_n.68, f32[2048]{0:T(1024)S(1)} %add_rsqrt_fusion), kind=kOutput, calls=%fused_computation.27 | convolution fusion | flops 1074790400 | bytes 11018244 | tf_op jit(solution)/shard_map/dot_general | solution.py:321
  86.0 10.0 %fusion = (f32[1024]{0:T(1024)S(1)}, f32[1024]{0:T(1024)S(1)}, f32[1024]{0:T(1024)S(1)}, f32[1024,2048]{1,0:T(8,128)}) fusion(f32[2048]{0:T(1024)S(1)} %bitcast.100, f32[2048]{0:T(1024)S(1)} %bitcast.98, pred[1024]{0:T(1024)(128)(4,1)S(1)} %fusion.51, f32[1024,2048]{1,0:T(8,128)S(1)} %fusion.8, f32[256,8192]{1,0:T(8,128)} %param.25, s32[]{:T(128)S(6)} %select_n.68, ...), kind=kOutput, calls=%fused_computation.7 | convolution fusion | flops 1091564544 | bytes 19436548 | tf_op jit(solution)/shard_map/dot_general | solution.py:323
  96.6 13.9 %shard_map.159 = f32[32,24,128]{2,1,0:T(8,128)} custom-call(f32[24,128]{1,0:T(8,128)} %reshape.158.refs_0_), custom_call_target="tpu_custom_call" | custom-call | bytes 786432 | tf_op jit(solution)/shard_map/pallas_call | solution.py:220
  112.9 7.6 %subtract_convert_fusion = bf16[1024,2048]{1,0:T(8,128)(2,1)S(1)} fusion(f32[1024,2048]{1,0:T(8,128)} %copy-done.1, f32[1024,2048]{1,0:T(8,128)} %get-tuple-element.42, f32[1024]{0:T(1024)S(1)} %get-tuple-element.38, f32[1024]{0:T(1024)S(1)} %get-tuple-element.37, f32[2048]{0:T(1024)S(1)} %bitcast.101, f32[2048]{0:T(1024)S(1)} %bitcast.99, ...), kind=kLoop, calls=%fused_computation.3 | loop fusion | flops 16777216 | bytes 20997120 | tf_op jit(solution)/shard_map/convert_element_type | solution.py:343
  120.5 3.9 %fusion.10 = f32[1024,256]{1,0:T(8,128)} fusion(bf16[1024,2048]{1,0:T(8,128)(2,1)S(1)} %subtract_convert_fusion, f32[256,8192]{1,0:T(8,128)} %param.24, s32[]{:T(128)S(6)} %select_n.68, f32[2048]{0:T(1024)S(1)} %add_rsqrt_fusion), kind=kOutput, calls=%fused_computation.32 | convolution fusion | flops 1074790400 | bytes 7348228 | tf_op jit(solution)/shard_map/dot_general | solution.py:344
  124.4 2.9 %multiply_reduce_fusion.1 = (f32[2048]{0:T(1024)S(1)}, f32[256,2048]{1,0:T(8,128)S(1)}) fusion(f32[256,8192]{1,0:T(8,128)} %param.24, s32[]{:T(128)S(6)} %select_n.68, f32[2048]{0:T(1024)S(1)} %add_rsqrt_fusion, bf16[1024,2048]{1,0:T(8,128)(2,1)S(1)} %subtract_convert_fusion, bf16[1024,512]{1,0:T(8,128)(2,1)S(1)} %bitcast.84), kind=kOutput, calls=%fused_computation.11 | convolution fusion | flops 1075312640 | bytes 8929284 | tf_op jit(solution)/shard_map/dot_general | solution.py:42
  127.3 2.1 %multiply_convert_fusion = bf16[256,2048]{1,0:T(8,128)(2,1)S(1)} fusion(f32[256,2048]{1,0:T(8,128)S(1)} %get-tuple-element.44, f32[256,8192]{1,0:T(8,128)} %param.24, s32[]{:T(128)S(6)} %select_n.68, f32[2048]{0:T(1024)S(1)} %get-tuple-element.43, f32[2048]{0:T(1024)S(1)} %add_rsqrt_fusion), kind=kLoop, calls=%fused_computation.10 | loop fusion | flops 2621440 | bytes 5259268 | tf_op jit(solution)/shard_map/convert_element_type | solution.py:355
  129.4 14.3 %shard_map.160 = f32[4,256,256]{2,1,0:T(8,128)} custom-call(f32[4,256,256]{2,1,0:T(8,128)} %bitcast.88), custom_call_target="tpu_custom_call" | custom-call | bytes 2097152 | tf_op jit(solution)/shard_map/pallas_call | solution.py:220
  143.7 2.0 %reduce_sum.164 = f32[256,256]{1,0:T(8,128)} reduce(f32[4,256,256]{2,1,0:T(8,128)} %shard_map.160, f32[]{:T(128)} %constant.23.clone.1), dimensions={0}, to_apply=%region_11.12 | reduce | flops 196608 | bytes 1310724 | tf_op jit(solution)/shard_map/reduce_sum | solution.py:354
  146.8 10.3 %shard_map.161 = (f32[8,32,256]{2,1,0:T(8,128)}, bf16[4,32,2048]{2,1,0:T(8,128)(2,1)}) custom-call(f32[8,32,256]{2,1,0:T(8,128)} %bitcast.87, bf16[4,32,2048]{2,1,0:T(8,128)(2,1)} %get-tuple-element.34.refs_1_), custom_call_target="tpu_custom_call" | custom-call | bytes 1572864 | tf_op jit(solution)/shard_map/pallas_call | solution.py:220
  158.9 10.0 %shard_map.162 = (bf16[8,32,256]{2,1,0:T(8,128)(2,1)}, bf16[4,32,2048]{2,1,0:T(8,128)(2,1)}) custom-call(bf16[32,256]{1,0:T(8,128)(2,1)} %multiply_convert_fusion.3.refs_0_, bf16[4,32,2048]{2,1,0:T(8,128)(2,1)} %get-tuple-element.33.refs_1_), custom_call_target="tpu_custom_call" | custom-call | bytes 1310720 | tf_op jit(solution)/shard_map/pallas_call | solution.py:220
  169.0 2.4 %convolution_convert_fusion = bf16[1536,256]{1,0:T(8,128)(2,1)} fusion(bf16[256,1536]{1,0:T(8,128)(2,1)S(1)} %bitcast.109, bf16[256,256]{1,0:T(8,128)(2,1)} %bitcast.96, bf16[256,256]{1,0:T(8,128)(2,1)S(1)} %copy-done.3, f32[256,256]{1,0:T(8,128)S(1)} %get-tuple-element.41), kind=kOutput, calls=%fused_computation.8 | convolution fusion | flops 235929600 | bytes 2097152 | tf_op jit(solution)/shard_map/dot_general | solution.py:42
  171.4 1.8 convolution_convert_fusion.1.refs_1_
  173.2 14.3 %shard_map.163 = (bf16[4,384,256]{2,1,0:T(8,128)(2,1)}, bf16[4,256,256]{2,1,0:T(8,128)(2,1)}) custom-call(bf16[4,384,256]{2,1,0:T(8,128)(2,1)} %bitcast.90, bf16[256,256]{1,0:T(8,128)(2,1)} %convolution_convert_fusion.1.refs_1_), custom_call_target="tpu_custom_call" | custom-call | bytes 2621440 | tf_op jit(solution)/shard_map/pallas_call | solution.py:220
  187.5 2.0 %convert_reduce_fusion = f32[384,256]{1,0:T(8,128)} fusion(bf16[4,384,256]{2,1,0:T(8,128)(2,1)} %get-tuple-element.26), kind=kLoop, calls=%fused_computation.17 | loop fusion | flops 688128 | bytes 1179648 | tf_op jit(solution)/shard_map/reduce_sum | solution.py:386
  189.5 1.8 convert_reduce_fusion.1
  (51 shorter events, 17.4 us)
Async XLA Ops:
  0.6 5.6 %copy-start = (bf16[1,256,1536]{2,1,0:T(8,128)(2,1)S(1)}, bf16[1,256,1536]{2,1,0:T(8,128)(2,1)}, u32[]{:S(2)}) copy-start(bf16[1,256,1536]{2,1,0:T(8,128)(2,1)} %param.16) | copy-start | bytes 2359300
  0.6 44.3 %copy-start.5 = (bf16[256,256]{1,0:T(8,128)(2,1)S(1)}, bf16[256,256]{1,0:T(8,128)(2,1)}, u32[]{:S(2)}) copy-start(bf16[256,256]{1,0:T(8,128)(2,1)} %param.23) | copy-start | bytes 393220
  8.8 40.0 %copy-start.3 = (bf16[256,256]{1,0:T(8,128)(2,1)S(1)}, bf16[256,256]{1,0:T(8,128)(2,1)}, u32[]{:S(2)}) copy-start(bf16[256,256]{1,0:T(8,128)(2,1)} %param.21) | copy-start | bytes 393220
  82.9 3.1 %copy-start.2 = (bf16[32,32,512]{2,1,0:T(8,128)(2,1)S(1)}, bf16[32,32,512]{2,1,0:T(8,128)(2,1)}, u32[]{:S(2)}) copy-start(bf16[32,32,512]{2,1,0:T(8,128)(2,1)} %shard_map.158) | copy-start | bytes 3145732
  86.0 10.0 %copy-start.1 = (f32[1024,2048]{1,0:T(8,128)}, f32[1024,2048]{1,0:T(8,128)S(1)}, u32[]{:S(2)}) copy-start(f32[1024,2048]{1,0:T(8,128)S(1)} %fusion.8) | copy-start | bytes 25165828
  127.3 41.7 %copy-start.4 = (bf16[8,32,1536]{2,1,0:T(8,128)(2,1)S(1)}, bf16[8,32,1536]{2,1,0:T(8,128)(2,1)}, u32[]{:S(2)}) copy-start(bf16[8,32,1536]{2,1,0:T(8,128)(2,1)} %get-tuple-element.17) | copy-start | bytes 2359300

commit v3 on v2

--- a/solution.py
+++ b/solution.py
@@ -234,6 +234,132 @@
     )(*[array for array, _, _ in jobs])
 
 
+def score_kernel(row_span, zs_ref, zt_ref, ps_ref, pt_ref, center_ref, es_ref, et_ref, sums_ref):
+    rows, share = es_ref.shape
+    chunk = min(512, share)
+    row = lax.broadcasted_iota(jnp.int32, (rows, 1), 0)
+    is_cls = lax.rem(row, row_span) == 0
+    total_t = jnp.zeros((rows, chunk), jnp.float32)
+    total_s = jnp.zeros((rows, chunk), jnp.float32)
+    cross = jnp.zeros((rows, chunk), jnp.float32)
+    for start in range(0, share, chunk):
+        here = pl.ds(start, chunk)
+        logit_s = jnp.dot(
+            zs_ref[...], ps_ref[:, here], preferred_element_type=jnp.float32
+        ) * (1.0 / student_temp)
+        shift = jnp.where(is_cls, center_ref[0:1, here], center_ref[1:2, here])
+        logit_t = (
+            jnp.dot(zt_ref[...], pt_ref[:, here], preferred_element_type=jnp.float32) - shift
+        ) * (1.0 / teacher_temp)
+        exp_s = jnp.exp(logit_s)
+        exp_t = jnp.exp(logit_t)
+        es_ref[:, here] = exp_s
+        et_ref[:, here] = exp_t
+        total_t += exp_t
+        total_s += exp_s
+        cross += exp_t * logit_s
+    lane = lax.broadcasted_iota(jnp.int32, (rows, 128), 1)
+    sums_ref[...] = jnp.where(
+        lane == 0,
+        jnp.sum(total_t, axis=1, keepdims=True),
+        jnp.where(
+            lane == 1,
+            jnp.sum(total_s, axis=1, keepdims=True),
+            jnp.sum(cross, axis=1, keepdims=True),
+        ),
+    )
+
+
+def scores(rows_s, rows_t, proto_s, proto_t, center, row_span):
+    rows, depth = rows_s.shape
+    share = proto_s.shape[1]
+    tile = math.gcd(rows, 8 * row_span)
+    return pl.pallas_call(
+        functools.partial(score_kernel, row_span),
+        grid=(rows // tile,),
+        out_shape=[
+            jax.ShapeDtypeStruct((rows, share), jnp.float32),
+            jax.ShapeDtypeStruct((rows, share), jnp.float32),
+            jax.ShapeDtypeStruct((rows, 128), jnp.float32),
+        ],
+        in_specs=[
+            pl.BlockSpec((tile, depth), lambda i: (i, 0)),
+            pl.BlockSpec((tile, depth), lambda i: (i, 0)),
+            pl.BlockSpec((depth, share), lambda i: (0, 0)),
+            pl.BlockSpec((depth, share), lambda i: (0, 0)),
+            pl.BlockSpec((2, share), lambda i: (0, 0)),
+        ],
+        out_specs=[
+            pl.BlockSpec((tile, share), lambda i: (i, 0)),
+            pl.BlockSpec((tile, share), lambda i: (i, 0)),
+            pl.BlockSpec((tile, 128), lambda i: (i, 0)),
+        ],
+        compiler_params=pltpu.CompilerParams(vmem_limit_bytes=48 * 2**20),
+    )(rows_s, rows_t, proto_s, proto_t, center)
+
+
+def gradient_kernel(
+    zs_ref, ps_ref, unit_ref, inverse_ref, es_ref, et_ref, scale_ref, units_ref, out_ref, cols_ref
+):
+    rows, share = es_ref.shape
+    chunk = min(512, share)
+    scale_s = scale_ref[:, 0:1]
+    scale_t = scale_ref[:, 1:2]
+    step = pl.program_id(0)
+
+    @pl.when(step == 0)
+    def _():
+        cols_ref[...] = jnp.zeros_like(cols_ref)
+
+    total = jnp.zeros(units_ref.shape, jnp.float32)
+    for start in range(0, share, chunk):
+        here = pl.ds(start, chunk)
+        dscore = (es_ref[:, here] * scale_s - et_ref[:, here] * scale_t).astype(jnp.bfloat16)
+        total += lax.dot_general(
+            dscore, ps_ref[:, here], (((1,), (1,)), ((), ())), preferred_element_type=jnp.float32
+        )
+        cols_ref[:, here] += contract_rows(zs_ref[...], dscore)
+    units_ref[...] = total
+
+    @pl.when(step == pl.num_programs(0) - 1)
+    def _():
+        for start in range(0, share, chunk):
+            here = pl.ds(start, chunk)
+            cols = cols_ref[:, here]
+            unit = unit_ref[:, here]
+            along = jnp.sum(unit * cols, axis=0, keepdims=True)
+            out_ref[:, here] = (inverse_ref[:, here] * (cols - unit * along)).astype(jnp.bfloat16)
+
+
+def gradients(rows_s, proto_s, proto_unit, col_inverse, exp_s, exp_t, scales, row_span):
+    rows, depth = rows_s.shape
+    share = proto_s.shape[1]
+    tile = math.gcd(rows, 8 * row_span)
+    return pl.pallas_call(
+        gradient_kernel,
+        grid=(rows // tile,),
+        out_shape=[
+            jax.ShapeDtypeStruct((rows, depth), jnp.float32),
+            jax.ShapeDtypeStruct((depth, share), jnp.bfloat16),
+        ],
+        in_specs=[
+            pl.BlockSpec((tile, depth), lambda i: (i, 0)),
+            pl.BlockSpec((depth, share), lambda i: (0, 0)),
+            pl.BlockSpec((depth, share), lambda i: (0, 0)),
+            pl.BlockSpec((1, share), lambda i: (0, 0)),
+            pl.BlockSpec((tile, share), lambda i: (i, 0)),
+            pl.BlockSpec((tile, share), lambda i: (i, 0)),
+            pl.BlockSpec((tile, 2), lambda i: (i, 0)),
+        ],
+        out_specs=[
+            pl.BlockSpec((tile, depth), lambda i: (i, 0)),
+            pl.BlockSpec((depth, share), lambda i: (0, 0)),
+        ],
+        scratch_shapes=[pltpu.VMEM((depth, share), jnp.float32)],
+        compiler_params=pltpu.CompilerParams(vmem_limit_bytes=48 * 2**20),
+    )(rows_s, proto_s, proto_unit, col_inverse, exp_s, exp_t, scales)
+
+
 def shards(
     student_cls,
     student_patches,
@@ -317,16 +443,8 @@
     proto_s_b = proto_unit.astype(jnp.bfloat16)
     proto_t_b = teacher_unit.astype(jnp.bfloat16)
     is_cls = jnp.arange(all_rows, dtype=jnp.int32) % row_span == 0
-    shift = jnp.where(is_cls[:, None], own_center[0][None, :], own_center[1][None, :])
-    logit_s = jnp.dot(rows_s, proto_s_b, preferred_element_type=jnp.float32) / student_temp
-    logit_t = (
-        jnp.dot(rows_t, proto_t_b, preferred_element_type=jnp.float32) - shift
-    ) / teacher_temp
-    exp_s = jnp.exp(logit_s)
-    exp_t = jnp.exp(logit_t)
-    sums = jnp.stack(
-        [jnp.sum(exp_t, axis=1), jnp.sum(exp_s, axis=1), jnp.sum(exp_t * logit_s, axis=1)]
-    )
+    exp_s, exp_t, sums = scores(rows_s, rows_t, proto_s_b, proto_t_b, own_center, row_span)
+    sums = sums[:, :3].T
     (sums,) = exchange(3, (sums.reshape(-1, 128), PROTO + DATA, True))
     total_t, total_s, cross = jnp.sum(sums, axis=0).reshape(3, all_rows)
     weights = jnp.where(is_cls, 1.0 / crops_total, 1.0 / (crops_total * masked_count)).astype(
@@ -338,21 +456,15 @@
         * data_ways
     ).reshape(1)
     factor = loss_scale / student_temp * weights
-    dscore = (
-        exp_s * (factor / total_s)[:, None] - exp_t * (factor / total_t)[:, None]
-    ).astype(jnp.bfloat16)
-    grad_units = lax.dot_general(
-        dscore, proto_s_b, (((1,), (1,)), ((), ())), preferred_element_type=jnp.float32
-    )
-    grad_cols = contract_rows(rows_s, dscore)
-    projected = col_inverse * (
-        grad_cols - proto_unit * jnp.sum(proto_unit * grad_cols, axis=0, keepdims=True)
+    scales = jnp.stack([factor / total_s, factor / total_t], axis=1)
+    grad_units, projected = gradients(
+        rows_s, proto_s_b, proto_unit, col_inverse, exp_s, exp_t, scales, row_span
     )
     (grad_units,) = exchange(
         4, (grad_units.reshape(data_ways, group_rows, bottleneck), DATA, False)
     )
     grad_units = jnp.sum(grad_units, axis=0).reshape(proto_ways, own_rows, bottleneck)
-    projected = projected.astype(jnp.bfloat16).reshape(
+    projected = projected.reshape(
         data_ways, bottleneck // data_ways, share
     )
     half = bottleneck // data_ways // 2

time: 196 us -> 188 us (0.959)
  matrix products: 29.6 us -> 9.46 us
  Pallas kernels: 124 us -> 140 us
  other arithmetic: 29.1 us -> 22.5 us
  local copies, waits for them, and re-layouts: 8.82 us -> 11.7 us
    dot_general x3 -> x0, matrix products: 16.9 us -> none  [the longest x1 9.96 us: shards(): jnp.dot(rows_t, proto_t_b, preferred_element_type=jnp.float32) - shift]
    pallas_call x0 -> x2, Pallas kernels: none -> 16 us  [the longest x1 9.15 us: gradients(): pl.pallas_call(gradient_kernel, grid=(rows // tile,), out_shape=[jax.Shap...]
    convert_element_type x2, other arithmetic: 9.74 us -> 5.92 us  [the longest x1 3.26 us: shards(): proto_s_b = proto_unit.astype(jnp.bfloat16)]
    dot_general x3 -> x2, matrix products: 7.11 us -> 3.34 us  [contract_rows(): lax.dot_general(left, right, (((0,), (0,)), ((), ())), preferred_element_...]
    unnamed x13 -> x37, local copies, waits for them, and re-layouts: 0.04 us -> 2.03 us
where the time goes in v3:
time: 188 us
  Pallas kernels  140 us (74%)
  other arithmetic  22.5 us (12%)
  local copies, waits for them, and re-layouts  11.7 us (6%)
  matrix products  9.46 us (5%)
  between operations  3.56 us (2%)
    pallas_call x8, Pallas kernels, exchange(): pl.pallas_call(functools.partial(exchange_kernel, tuple(((axes, gather) f...  124 us
    pallas_call x1, Pallas kernels, gradients(): pl.pallas_call(gradient_kernel, grid=(rows // tile,), out_shape=[jax.Shap...  9.15 us
    pallas_call x1, Pallas kernels, scores(): pl.pallas_call(functools.partial(score_kernel, row_span), grid=(rows // t...  6.86 us

profile of v3, /device:TPU:0, one launch (start us, length us, event | category | flops | bytes accessed | tf_op | source)
XLA Modules:
  0.0 187.6 jit_solution(7869750077041161175)
XLA Ops:
  2.7 1.8 multiply_reduce_fusion
  7.9 2.7 %multiply_convert_fusion = (bf16[256,2048]{1,0:T(8,128)(2,1)S(1)}, f32[2048]{0:T(1024)S(1)}) fusion(f32[256,8192]{1,0:T(8,128)} %param.25, s32[]{:T(128)S(6)} %select_n.67, f32[2048]{0:T(1024)S(1)} %add_rsqrt_fusion, f32[256,8192]{1,0:T(8,128)} %param.24), kind=kLoop, calls=%fused_computation.5 | loop fusion | flops 2095104 | bytes 5259268 | tf_op jit(solution)/shard_map/convert_element_type | solution.py:444
  10.5 31.5 %shard_map.156 = (bf16[8,32,1536]{2,1,0:T(8,128)(2,1)}, bf16[8,32,1536]{2,1,0:T(8,128)(2,1)}, s32[8,1,8,128]{3,2,1,0:T(8,128)}, bf16[4,384,256]{2,1,0:T(8,128)(2,1)}, bf16[4,384,256]{2,1,0:T(8,128)(2,1)}) custom-call(bf16[32,1536]{1,0:T(8,128)(2,1)} %get-tuple-element.50.refs_0_, bf16[32,1536]{1,0:T(8,128)(2,1)} %get-tuple-element.51.refs_1_, ...), custom_call_target="tpu_custom_call" | custom-call | bytes 6356992 | tf_op jit(solution)/shard_map/pallas_call | solution.py:220
  42.1 3.0 %fusion.3 = (bf16[256,256]{1,0:T(8,128)(2,1)S(1)}, f32[256,256]{1,0:T(8,128)}) fusion(bf16[256,1536]{1,0:T(8,128)(2,1)} %bitcast.84, bf16[1536,256]{1,0:T(8,128)(2,1)} %bitcast.88), kind=kOutput, calls=%fused_computation.20 | convolution fusion | flops 205586432 | bytes 1966080 | tf_op jit(solution)/shard_map/dot_general | solution.py:409
  45.1 1.0 slice_reduce_fusion
  46.1 2.2 %fusion.35 = bf16[256,256]{1,0:T(8,128)(2,1)S(1)} fusion(bf16[256,256]{1,0:T(8,128)(2,1)S(1)} %copy-done.16, bf16[256,1536]{1,0:T(8,128)(2,1)S(1)} %bitcast.86, bf16[1536,256]{1,0:T(8,128)(2,1)} %bitcast.87), kind=kOutput, calls=%fused_computation.70 | convolution fusion | flops 239140864 | bytes 1835008 | tf_op jit(solution)/shard_map/dot_general | solution.py:418
  50.6 14.9 %shard_map.157 = (f32[8,32,256]{2,1,0:T(8,128)}, bf16[8,32,256]{2,1,0:T(8,128)(2,1)}) custom-call(f32[8,32,256]{2,1,0:T(8,128)} %bitcast.70, bf16[8,32,256]{2,1,0:T(8,128)(2,1)} %pad_maximum_fusion.refs_1_), custom_call_target="tpu_custom_call" | custom-call | bytes 786432 | tf_op jit(solution)/shard_map/pallas_call | solution.py:220
  68.4 15.4 %shard_map.158 = bf16[32,32,512]{2,1,0:T(8,128)(2,1)} custom-call(bf16[32,512]{1,0:T(8,128)(2,1)} %pad_maximum_fusion.1.refs_0_), custom_call_target="tpu_custom_call" | custom-call | bytes 2097152 | tf_op jit(solution)/shard_map/pallas_call | solution.py:220
  83.8 1.3 fusion.86
  85.0 3.3 %fusion.84 = (bf16[256,2048]{1,0:T(8,128)(2,1)S(1)}, f32[256,2048]{1,0:T(8,128)}) fusion(f32[2048]{0:T(1024)S(1)} %add_rsqrt_fusion.1, f32[256,8192]{1,0:T(8,128)} %param.24, s32[]{:T(128)S(6)} %select_n.67), kind=kLoop, calls=%fused_computation.147 | loop fusion | flops 1048576 | bytes 5251076 | tf_op jit(solution)/shard_map/convert_element_type | solution.py:443
  88.3 6.9 %shard_map.159 = (f32[1024,2048]{1,0:T(8,128)}, f32[1024,2048]{1,0:T(8,128)}, f32[1024,128]{1,0:T(8,128)S(1)}) custom-call(bf16[1024,256]{1,0:T(8,128)(2,1)S(1)} %get-tuple-element.45.zs_ref, bf16[1024,256]{1,0:T(8,128)(2,1)S(1)} %get-tuple-element.44.zt_ref, bf16[256,2048]{1,0:T(8,128)(2,1)S(1)} %get-tuple-element.40.ps_ref, ...), custom_call_target="tpu_custom_call" | custom-call | tf_op jit(solution)/shard_map/pallas_call | solution.py:277
  96.0 13.9 %shard_map.160 = f32[32,24,128]{2,1,0:T(8,128)} custom-call(f32[24,128]{1,0:T(8,128)} %reshape.195.refs_0_), custom_call_target="tpu_custom_call" | custom-call | bytes 786432 | tf_op jit(solution)/shard_map/pallas_call | solution.py:220
  109.9 1.0 reduce_sum.123
  112.6 9.1 %shard_map.161 = (f32[1024,256]{1,0:T(8,128)S(1)}, bf16[256,2048]{1,0:T(8,128)(2,1)S(1)}) custom-call(bf16[1024,256]{1,0:T(8,128)(2,1)S(1)} %get-tuple-element.45.zs_ref, bf16[256,2048]{1,0:T(8,128)(2,1)S(1)} %get-tuple-element.40.ps_ref, f32[256,2048]{1,0:T(8,128)} %get-tuple-element.41.unit_ref, f32[1,2048]{1,0:T(1,128)S(1)} %bitcast.66, ...), custom_call_target="tpu_custom_call" | custom-call | tf_op jit(solution)/shard_map/pallas_call | solution.py:338
  123.7 14.2 %shard_map.162 = f32[4,256,256]{2,1,0:T(8,128)} custom-call(f32[4,256,256]{2,1,0:T(8,128)} %bitcast.65), custom_call_target="tpu_custom_call" | custom-call | bytes 2097152 | tf_op jit(solution)/shard_map/pallas_call | solution.py:220
  137.9 2.0 %reduce_sum.125 = f32[256,256]{1,0:T(8,128)} reduce(f32[4,256,256]{2,1,0:T(8,128)} %shard_map.162, f32[]{:T(128)} %constant.21.clone.1), dimensions={0}, to_apply=%region_8.9 | reduce | flops 196608 | bytes 1310724 | tf_op jit(solution)/shard_map/reduce_sum | solution.py:466
  139.9 1.0 fusion.85
  140.9 10.4 %shard_map.163 = (f32[8,32,256]{2,1,0:T(8,128)}, bf16[4,32,2048]{2,1,0:T(8,128)(2,1)}) custom-call(f32[8,32,256]{2,1,0:T(8,128)} %bitcast.69, bf16[4,32,2048]{2,1,0:T(8,128)(2,1)} %get-tuple-element.43.refs_1_), custom_call_target="tpu_custom_call" | custom-call | bytes 1572864 | tf_op jit(solution)/shard_map/pallas_call | solution.py:220
  153.2 10.0 %shard_map.164 = (bf16[8,32,256]{2,1,0:T(8,128)(2,1)}, bf16[4,32,2048]{2,1,0:T(8,128)(2,1)}) custom-call(bf16[32,256]{1,0:T(8,128)(2,1)} %multiply_convert_fusion.1.refs_0_, bf16[4,32,2048]{2,1,0:T(8,128)(2,1)} %get-tuple-element.42.refs_1_), custom_call_target="tpu_custom_call" | custom-call | bytes 1310720 | tf_op jit(solution)/shard_map/pallas_call | solution.py:220
  163.2 2.5 %convolution_convert_fusion = bf16[1536,256]{1,0:T(8,128)(2,1)} fusion(bf16[256,1536]{1,0:T(8,128)(2,1)S(1)} %bitcast.85, bf16[256,256]{1,0:T(8,128)(2,1)} %bitcast.77, bf16[256,256]{1,0:T(8,128)(2,1)S(1)} %copy-done.11, f32[256,256]{1,0:T(8,128)S(1)} %copy-done.17), kind=kOutput, calls=%fused_computation.3 | convolution fusion | flops 235929600 | bytes 2097152 | tf_op jit(solution)/shard_map/dot_general | solution.py:42
  166.6 14.3 %shard_map.165 = (bf16[4,384,256]{2,1,0:T(8,128)(2,1)}, bf16[4,256,256]{2,1,0:T(8,128)(2,1)}) custom-call(bf16[4,384,256]{2,1,0:T(8,128)(2,1)} %bitcast.71, bf16[256,256]{1,0:T(8,128)(2,1)} %convolution_convert_fusion.1.refs_1_), custom_call_target="tpu_custom_call" | custom-call | bytes 2621440 | tf_op jit(solution)/shard_map/pallas_call | solution.py:220
  180.9 2.0 %convert_reduce_fusion = f32[384,256]{1,0:T(8,128)} fusion(bf16[4,384,256]{2,1,0:T(8,128)(2,1)} %get-tuple-element.36), kind=kLoop, calls=%fused_computation.9 | loop fusion | flops 688128 | bytes 1179648 | tf_op jit(solution)/shard_map/reduce_sum | solution.py:498
  182.9 1.8 convert_reduce_fusion.1
  185.0 1.5 copy.28
  (79 shorter events, 16.6 us)
Async XLA Ops:
  0.6 4.6 %copy-start = (bf16[1,256,1536]{2,1,0:T(8,128)(2,1)S(1)}, bf16[1,256,1536]{2,1,0:T(8,128)(2,1)}, u32[]{:S(2)}) copy-start(bf16[1,256,1536]{2,1,0:T(8,128)(2,1)} %param.16) | copy-start | bytes 2359300
  0.6 6.5 %copy-start.13 = (bf16[1,1536]{1,0:T(2,128)(2,1)S(1)}, bf16[1,1536]{1,0:T(2,128)(2,1)}, u32[]{:S(2)}) copy-start(bf16[1,1536]{1,0:T(2,128)(2,1)} %param.15) | copy-start | bytes 9220
  0.7 5.5 %copy-start.4 = (bf16[1,256,1536]{2,1,0:T(8,128)(2,1)S(1)}, bf16[1,256,1536]{2,1,0:T(8,128)(2,1)}, u32[]{:S(2)}) copy-start(bf16[1,256,1536]{2,1,0:T(8,128)(2,1)} %param.14) | copy-start | bytes 2359300
  0.7 6.4 %copy-start.12 = (bf16[1,1536]{1,0:T(2,128)(2,1)S(1)}, bf16[1,1536]{1,0:T(2,128)(2,1)}, u32[]{:S(2)}) copy-start(bf16[1,1536]{1,0:T(2,128)(2,1)} %param.13) | copy-start | bytes 9220
  42.0 4.0 %copy-start.15 = (bf16[8,32,1536]{2,1,0:T(8,128)(2,1)S(1)}, bf16[8,32,1536]{2,1,0:T(8,128)(2,1)}, u32[]{:S(2)}) copy-start(bf16[8,32,1536]{2,1,0:T(8,128)(2,1)} %get-tuple-element.24) | copy-start | bytes 2359300
  42.0 4.0 %copy-start.16 = (bf16[256,256]{1,0:T(8,128)(2,1)S(1)}, bf16[256,256]{1,0:T(8,128)(2,1)}, u32[]{:S(2)}) copy-start(bf16[256,256]{1,0:T(8,128)(2,1)} %param.23) | copy-start | bytes 393220
  45.0 4.6 %copy-start.5 = (bf16[256,256]{1,0:T(8,128)(2,1)}, bf16[256,256]{1,0:T(8,128)(2,1)S(1)}, u32[]{:S(2)}) copy-start(bf16[256,256]{1,0:T(8,128)(2,1)S(1)} %get-tuple-element.48) | copy-start | bytes 393220
  46.1 3.6 %copy-start.10 = (bf16[256,256]{1,0:T(8,128)(2,1)S(1)}, bf16[256,256]{1,0:T(8,128)(2,1)}, u32[]{:S(2)}) copy-start(bf16[256,256]{1,0:T(8,128)(2,1)} %param.21) | copy-start | bytes 393220
  121.7 1.0 copy-start.1
  122.7 1.0 copy-start.3
  123.7 16.2 %copy-start.2 = (bf16[256,2048]{1,0:T(8,128)(2,1)S(1)}, bf16[256,2048]{1,0:T(8,128)(2,1)}, u32[]{:S(2)}) copy-start(bf16[256,2048]{1,0:T(8,128)(2,1)} %copy-done.1) | copy-start | bytes 3145732
  139.9 23.3 %copy-start.11 = (bf16[256,256]{1,0:T(8,128)(2,1)S(1)}, bf16[256,256]{1,0:T(8,128)(2,1)}, u32[]{:S(2)}) copy-start(bf16[256,256]{1,0:T(8,128)(2,1)} %param.21) | copy-start | bytes 393220
  139.9 23.3 %copy-start.14 = (bf16[8,32,1536]{2,1,0:T(8,128)(2,1)S(1)}, bf16[8,32,1536]{2,1,0:T(8,128)(2,1)}, u32[]{:S(2)}) copy-start(bf16[8,32,1536]{2,1,0:T(8,128)(2,1)} %get-tuple-element.22) | copy-start | bytes 2359300
  139.9 23.3 %copy-start.17 = (f32[256,256]{1,0:T(8,128)S(1)}, f32[256,256]{1,0:T(8,128)}, u32[]{:S(2)}) copy-start(f32[256,256]{1,0:T(8,128)} %get-tuple-element.49) | copy-start | bytes 786436
  140.9 24.7 %copy-start.6 = (bf16[256,256]{1,0:T(8,128)(2,1)S(1)}, bf16[256,256]{1,0:T(8,128)(2,1)}, u32[]{:S(2)}) copy-start(bf16[256,256]{1,0:T(8,128)(2,1)} %copy-done.5) | copy-start | bytes 393220
  163.2 2.5 %copy-start.9 = (bf16[8,32,256]{2,1,0:T(8,128)(2,1)S(1)}, bf16[8,32,256]{2,1,0:T(8,128)(2,1)}, u32[]{:S(2)}) copy-start(bf16[8,32,256]{2,1,0:T(8,128)(2,1)} %get-tuple-element.35) | copy-start | bytes 393220
  165.7 19.0 %copy-start.7 = (bf16[4,32,2048]{2,1,0:T(8,128)(2,1)S(1)}, bf16[4,32,2048]{2,1,0:T(8,128)(2,1)}, u32[]{:S(2)}) copy-start(bf16[4,32,2048]{2,1,0:T(8,128)(2,1)} %get-tuple-element.38) | copy-start | bytes 1572868
  165.7 19.0 %copy-start.8 = (bf16[4,32,2048]{2,1,0:T(8,128)(2,1)S(1)}, bf16[4,32,2048]{2,1,0:T(8,128)(2,1)}, u32[]{:S(2)}) copy-start(bf16[4,32,2048]{2,1,0:T(8,128)(2,1)} %get-tuple-element.39) | copy-start | bytes 1572868

commit v4 on v3

--- a/solution.py
+++ b/solution.py
@@ -270,9 +270,9 @@
     )
 
 
-def scores(rows_s, rows_t, proto_s, proto_t, center, row_span):
-    rows, depth = rows_s.shape
-    share = proto_s.shape[1]
+def scores(units, proto_s, proto_t, center, row_span):
+    rows = units.shape[0]
+    depth, share = proto_s.shape
     tile = math.gcd(rows, 8 * row_span)
     return pl.pallas_call(
         functools.partial(score_kernel, row_span),
@@ -284,7 +284,7 @@
         ],
         in_specs=[
             pl.BlockSpec((tile, depth), lambda i: (i, 0)),
-            pl.BlockSpec((tile, depth), lambda i: (i, 0)),
+            pl.BlockSpec((tile, depth), lambda i: (i, 1)),
             pl.BlockSpec((depth, share), lambda i: (0, 0)),
             pl.BlockSpec((depth, share), lambda i: (0, 0)),
             pl.BlockSpec((2, share), lambda i: (0, 0)),
@@ -295,7 +295,7 @@
             pl.BlockSpec((tile, 128), lambda i: (i, 0)),
         ],
         compiler_params=pltpu.CompilerParams(vmem_limit_bytes=48 * 2**20),
-    )(rows_s, rows_t, proto_s, proto_t, center)
+    )(units, units, proto_s, proto_t, center)
 
 
 def gradient_kernel(
@@ -331,9 +331,9 @@
             out_ref[:, here] = (inverse_ref[:, here] * (cols - unit * along)).astype(jnp.bfloat16)
 
 
-def gradients(rows_s, proto_s, proto_unit, col_inverse, exp_s, exp_t, scales, row_span):
-    rows, depth = rows_s.shape
-    share = proto_s.shape[1]
+def gradients(units, proto_s, proto_unit, col_inverse, exp_s, exp_t, scales, row_span):
+    rows = units.shape[0]
+    depth, share = proto_s.shape
     tile = math.gcd(rows, 8 * row_span)
     return pl.pallas_call(
         gradient_kernel,
@@ -357,7 +357,7 @@
         ],
         scratch_shapes=[pltpu.VMEM((depth, share), jnp.float32)],
         compiler_params=pltpu.CompilerParams(vmem_limit_bytes=48 * 2**20),
-    )(rows_s, proto_s, proto_unit, col_inverse, exp_s, exp_t, scales)
+    )(units, proto_s, proto_unit, col_inverse, exp_s, exp_t, scales)
 
 
 def shards(
@@ -432,8 +432,6 @@
     packed = jnp.concatenate([unit_s, unit_t], axis=1).astype(jnp.bfloat16)
     (all_units,) = exchange(2, (packed, PROTO + DATA, True))
     all_units = all_units.reshape(all_rows, 2 * bottleneck)
-    rows_s = all_units[:, :bottleneck]
-    rows_t = all_units[:, bottleneck:]
 
     own_s = lax.dynamic_slice_in_dim(student_proto, data_index * share, share, axis=1)
     own_t = lax.dynamic_slice_in_dim(teacher_proto, data_index * share, share, axis=1)
@@ -443,7 +441,7 @@
     proto_s_b = proto_unit.astype(jnp.bfloat16)
     proto_t_b = teacher_unit.astype(jnp.bfloat16)
     is_cls = jnp.arange(all_rows, dtype=jnp.int32) % row_span == 0
-    exp_s, exp_t, sums = scores(rows_s, rows_t, proto_s_b, proto_t_b, own_center, row_span)
+    exp_s, exp_t, sums = scores(all_units, proto_s_b, proto_t_b, own_center, row_span)
     sums = sums[:, :3].T
     (sums,) = exchange(3, (sums.reshape(-1, 128), PROTO + DATA, True))
     total_t, total_s, cross = jnp.sum(sums, axis=0).reshape(3, all_rows)
@@ -458,7 +456,7 @@
     factor = loss_scale / student_temp * weights
     scales = jnp.stack([factor / total_s, factor / total_t], axis=1)
     grad_units, projected = gradients(
-        rows_s, proto_s_b, proto_unit, col_inverse, exp_s, exp_t, scales, row_span
+        all_units, proto_s_b, proto_unit, col_inverse, exp_s, exp_t, scales, row_span
     )
     (grad_units,) = exchange(
         4, (grad_units.reshape(data_ways, group_rows, bottleneck), DATA, False)

time: 188 us -> 187 us (level)
  no operation moved by 1% of the time
where the time goes in v4:
time: 187 us; the launch traced here: 186 us
  Pallas kernels  140 us (75%)
  other arithmetic  23.6 us (13%)
  local copies, waits for them, and re-layouts  10.4 us (6%)
  matrix products  8.35 us (4%)
  between operations  3.57 us (2%)
    pallas_call x8, Pallas kernels, exchange(): pl.pallas_call(functools.partial(exchange_kernel, tuple(((axes, gather) f...  124 us
    pallas_call x1, Pallas kernels, gradients(): pl.pallas_call(gradient_kernel, grid=(rows // tile,), out_shape=[jax.Shap...  9.13 us
    pallas_call x1, Pallas kernels, scores(): pl.pallas_call(functools.partial(score_kernel, row_span), grid=(rows // t...  6.96 us

profile of v4, /device:TPU:0, one launch (start us, length us, event | category | flops | bytes accessed | tf_op | source)
XLA Modules:
  0.0 186.4 jit_solution(15377716534694767136)
XLA Ops:
  2.7 1.8 multiply_reduce_fusion
  7.9 3.6 %multiply_convert_fusion = (bf16[256,2048]{1,0:T(8,128)(2,1)}, f32[2048]{0:T(1024)S(1)}) fusion(f32[256,8192]{1,0:T(8,128)} %param.25, s32[]{:T(128)S(6)} %select_n.67, f32[2048]{0:T(1024)S(1)} %add_rsqrt_fusion, f32[256,8192]{1,0:T(8,128)} %param.24), kind=kLoop, calls=%fused_computation.5 | loop fusion | flops 2095104 | bytes 5259268 | tf_op jit(solution)/shard_map/convert_element_type | solution.py:442
  11.5 31.4 %shard_map.156 = (bf16[8,32,1536]{2,1,0:T(8,128)(2,1)}, bf16[8,32,1536]{2,1,0:T(8,128)(2,1)}, s32[8,1,8,128]{3,2,1,0:T(8,128)}, bf16[4,384,256]{2,1,0:T(8,128)(2,1)}, bf16[4,384,256]{2,1,0:T(8,128)(2,1)}) custom-call(bf16[32,1536]{1,0:T(8,128)(2,1)} %get-tuple-element.48.refs_0_, bf16[32,1536]{1,0:T(8,128)(2,1)} %get-tuple-element.49.refs_1_, ...), custom_call_target="tpu_custom_call" | custom-call | bytes 6356992 | tf_op jit(solution)/shard_map/pallas_call | solution.py:220
  42.9 3.0 %fusion.3 = (bf16[256,256]{1,0:T(8,128)(2,1)S(1)}, f32[256,256]{1,0:T(8,128)}) fusion(bf16[256,1536]{1,0:T(8,128)(2,1)} %bitcast.86, bf16[1536,256]{1,0:T(8,128)(2,1)} %bitcast.90), kind=kOutput, calls=%fused_computation.20 | convolution fusion | flops 205586432 | bytes 1966080 | tf_op jit(solution)/shard_map/dot_general | solution.py:409
  46.0 1.0 slice_reduce_fusion
  47.0 1.1 fusion.35
  50.4 14.9 %shard_map.157 = (f32[8,32,256]{2,1,0:T(8,128)}, bf16[8,32,256]{2,1,0:T(8,128)(2,1)}) custom-call(f32[8,32,256]{2,1,0:T(8,128)} %bitcast.72, bf16[8,32,256]{2,1,0:T(8,128)(2,1)} %pad_maximum_fusion.refs_1_), custom_call_target="tpu_custom_call" | custom-call | bytes 786432 | tf_op jit(solution)/shard_map/pallas_call | solution.py:220
  68.2 15.4 %shard_map.158 = bf16[32,32,512]{2,1,0:T(8,128)(2,1)} custom-call(bf16[32,512]{1,0:T(8,128)(2,1)} %pad_maximum_fusion.1.refs_0_), custom_call_target="tpu_custom_call" | custom-call | bytes 2097152 | tf_op jit(solution)/shard_map/pallas_call | solution.py:220
  83.6 3.4 %fusion.84 = (bf16[256,2048]{1,0:T(8,128)(2,1)S(1)}, f32[256,2048]{1,0:T(8,128)}) fusion(f32[2048]{0:T(1024)S(1)} %add_rsqrt_fusion.1, f32[256,8192]{1,0:T(8,128)} %param.24, s32[]{:T(128)S(6)} %select_n.67), kind=kLoop, calls=%fused_computation.147 | loop fusion | flops 1048576 | bytes 5251076 | tf_op jit(solution)/shard_map/convert_element_type | solution.py:441
  87.0 7.0 %shard_map.159 = (f32[1024,2048]{1,0:T(8,128)}, f32[1024,2048]{1,0:T(8,128)}, f32[1024,128]{1,0:T(8,128)S(1)}) custom-call(bf16[1024,512]{1,0:T(8,128)(2,1)S(1)} %bitcast.64, bf16[1024,512]{1,0:T(8,128)(2,1)S(1)} %bitcast.65, bf16[256,2048]{1,0:T(8,128)(2,1)S(1)} %get-tuple-element.40.ps_ref, bf16[256,2048]{1,0:T(8,128)(2,1)S(1)} %copy-done.2, ...), custom_call_target="tpu_custom_call" | custom-call | tf_op jit(solution)/shard_map/pallas_call | solution.py:277
  94.8 13.9 %shard_map.160 = f32[32,24,128]{2,1,0:T(8,128)} custom-call(f32[24,128]{1,0:T(8,128)} %reshape.195.refs_0_), custom_call_target="tpu_custom_call" | custom-call | bytes 786432 | tf_op jit(solution)/shard_map/pallas_call | solution.py:220
  108.7 1.0 reduce_sum.123
  111.4 9.1 %shard_map.161 = (f32[1024,256]{1,0:T(8,128)S(1)}, bf16[256,2048]{1,0:T(8,128)(2,1)S(1)}) custom-call(bf16[1024,512]{1,0:T(8,128)(2,1)S(1)} %bitcast.66, bf16[256,2048]{1,0:T(8,128)(2,1)S(1)} %get-tuple-element.40.ps_ref, f32[256,2048]{1,0:T(8,128)} %get-tuple-element.41.unit_ref, f32[1,2048]{1,0:T(1,128)S(1)} %bitcast.69, ...), custom_call_target="tpu_custom_call" | custom-call | tf_op jit(solution)/shard_map/pallas_call | solution.py:338
  120.5 1.0 copy-done.3
  122.5 14.2 %shard_map.162 = f32[4,256,256]{2,1,0:T(8,128)} custom-call(f32[4,256,256]{2,1,0:T(8,128)} %bitcast.68), custom_call_target="tpu_custom_call" | custom-call | bytes 2097152 | tf_op jit(solution)/shard_map/pallas_call | solution.py:220
  136.7 2.0 %reduce_sum.125 = f32[256,256]{1,0:T(8,128)} reduce(f32[4,256,256]{2,1,0:T(8,128)} %shard_map.162, f32[]{:T(128)} %constant.21.clone.1), dimensions={0}, to_apply=%region_8.9 | reduce | flops 196608 | bytes 1310724 | tf_op jit(solution)/shard_map/reduce_sum | solution.py:464
  138.7 1.0 fusion.85
  139.7 10.3 %shard_map.163 = (f32[8,32,256]{2,1,0:T(8,128)}, bf16[4,32,2048]{2,1,0:T(8,128)(2,1)}) custom-call(f32[8,32,256]{2,1,0:T(8,128)} %bitcast.71, bf16[4,32,2048]{2,1,0:T(8,128)(2,1)} %get-tuple-element.43.refs_1_), custom_call_target="tpu_custom_call" | custom-call | bytes 1572864 | tf_op jit(solution)/shard_map/pallas_call | solution.py:220
  151.9 10.0 %shard_map.164 = (bf16[8,32,256]{2,1,0:T(8,128)(2,1)}, bf16[4,32,2048]{2,1,0:T(8,128)(2,1)}) custom-call(bf16[32,256]{1,0:T(8,128)(2,1)} %multiply_convert_fusion.1.refs_0_, bf16[4,32,2048]{2,1,0:T(8,128)(2,1)} %get-tuple-element.42.refs_1_), custom_call_target="tpu_custom_call" | custom-call | bytes 1310720 | tf_op jit(solution)/shard_map/pallas_call | solution.py:220
  162.0 2.5 %convolution_convert_fusion = bf16[1536,256]{1,0:T(8,128)(2,1)} fusion(bf16[256,1536]{1,0:T(8,128)(2,1)S(1)} %bitcast.87, bf16[256,256]{1,0:T(8,128)(2,1)} %bitcast.79, bf16[256,256]{1,0:T(8,128)(2,1)S(1)} %copy-done.13, f32[256,256]{1,0:T(8,128)S(1)} %copy-done.20), kind=kOutput, calls=%fused_computation.3 | convolution fusion | flops 235929600 | bytes 2097152 | tf_op jit(solution)/shard_map/dot_general | solution.py:42
  165.4 14.3 %shard_map.165 = (bf16[4,384,256]{2,1,0:T(8,128)(2,1)}, bf16[4,256,256]{2,1,0:T(8,128)(2,1)}) custom-call(bf16[4,384,256]{2,1,0:T(8,128)(2,1)} %bitcast.73, bf16[256,256]{1,0:T(8,128)(2,1)} %convolution_convert_fusion.1.refs_1_), custom_call_target="tpu_custom_call" | custom-call | bytes 2621440 | tf_op jit(solution)/shard_map/pallas_call | solution.py:220
  179.7 2.0 %convert_reduce_fusion = f32[384,256]{1,0:T(8,128)} fusion(bf16[4,384,256]{2,1,0:T(8,128)(2,1)} %get-tuple-element.36), kind=kLoop, calls=%fused_computation.9 | loop fusion | flops 688128 | bytes 1179648 | tf_op jit(solution)/shard_map/reduce_sum | solution.py:496
  181.7 1.8 convert_reduce_fusion.1
  183.8 1.5 copy.28
  (84 shorter events, 15.6 us)
Async XLA Ops:
  0.6 4.6 %copy-start = (bf16[1,256,1536]{2,1,0:T(8,128)(2,1)S(1)}, bf16[1,256,1536]{2,1,0:T(8,128)(2,1)}, u32[]{:S(2)}) copy-start(bf16[1,256,1536]{2,1,0:T(8,128)(2,1)} %param.16) | copy-start | bytes 2359300
  0.6 6.5 %copy-start.15 = (bf16[1,1536]{1,0:T(2,128)(2,1)S(1)}, bf16[1,1536]{1,0:T(2,128)(2,1)}, u32[]{:S(2)}) copy-start(bf16[1,1536]{1,0:T(2,128)(2,1)} %param.15) | copy-start | bytes 9220
  0.7 5.5 %copy-start.6 = (bf16[1,256,1536]{2,1,0:T(8,128)(2,1)S(1)}, bf16[1,256,1536]{2,1,0:T(8,128)(2,1)}, u32[]{:S(2)}) copy-start(bf16[1,256,1536]{2,1,0:T(8,128)(2,1)} %param.14) | copy-start | bytes 2359300
  0.7 6.4 %copy-start.14 = (bf16[1,1536]{1,0:T(2,128)(2,1)S(1)}, bf16[1,1536]{1,0:T(2,128)(2,1)}, u32[]{:S(2)}) copy-start(bf16[1,1536]{1,0:T(2,128)(2,1)} %param.13) | copy-start | bytes 9220
  42.9 4.1 %copy-start.17 = (bf16[8,32,1536]{2,1,0:T(8,128)(2,1)S(1)}, bf16[8,32,1536]{2,1,0:T(8,128)(2,1)}, u32[]{:S(2)}) copy-start(bf16[8,32,1536]{2,1,0:T(8,128)(2,1)} %get-tuple-element.24) | copy-start | bytes 2359300
  42.9 4.1 %copy-start.18 = (bf16[4,384,256]{2,1,0:T(8,128)(2,1)S(1)}, bf16[4,384,256]{2,1,0:T(8,128)(2,1)}, u32[]{:S(2)}) copy-start(bf16[4,384,256]{2,1,0:T(8,128)(2,1)} %get-tuple-element.25) | copy-start | bytes 2359300
  42.9 4.1 %copy-start.19 = (bf16[256,256]{1,0:T(8,128)(2,1)S(1)}, bf16[256,256]{1,0:T(8,128)(2,1)}, u32[]{:S(2)}) copy-start(bf16[256,256]{1,0:T(8,128)(2,1)} %param.23) | copy-start | bytes 393220
  46.0 3.5 %copy-start.7 = (bf16[256,256]{1,0:T(8,128)(2,1)}, bf16[256,256]{1,0:T(8,128)(2,1)S(1)}, u32[]{:S(2)}) copy-start(bf16[256,256]{1,0:T(8,128)(2,1)S(1)} %get-tuple-element.46) | copy-start | bytes 393220
  47.0 2.5 %copy-start.12 = (bf16[256,256]{1,0:T(8,128)(2,1)S(1)}, bf16[256,256]{1,0:T(8,128)(2,1)}, u32[]{:S(2)}) copy-start(bf16[256,256]{1,0:T(8,128)(2,1)} %param.21) | copy-start | bytes 393220
  83.6 3.4 %copy-start.1 = (bf16[32,32,512]{2,1,0:T(8,128)(2,1)S(1)}, bf16[32,32,512]{2,1,0:T(8,128)(2,1)}, u32[]{:S(2)}) copy-start(bf16[32,32,512]{2,1,0:T(8,128)(2,1)} %shard_map.158) | copy-start | bytes 3145732
  83.6 3.4 %copy-start.2 = (bf16[256,2048]{1,0:T(8,128)(2,1)S(1)}, bf16[256,2048]{1,0:T(8,128)(2,1)}, u32[]{:S(2)}) copy-start(bf16[256,2048]{1,0:T(8,128)(2,1)} %get-tuple-element.50.pt_ref) | copy-start | bytes 3145732
  120.5 1.0 copy-start.3
  121.5 1.0 copy-start.5
  122.5 16.2 %copy-start.4 = (bf16[256,2048]{1,0:T(8,128)(2,1)S(1)}, bf16[256,2048]{1,0:T(8,128)(2,1)}, u32[]{:S(2)}) copy-start(bf16[256,2048]{1,0:T(8,128)(2,1)} %copy-done.3) | copy-start | bytes 3145732
  138.7 23.3 %copy-start.13 = (bf16[256,256]{1,0:T(8,128)(2,1)S(1)}, bf16[256,256]{1,0:T(8,128)(2,1)}, u32[]{:S(2)}) copy-start(bf16[256,256]{1,0:T(8,128)(2,1)} %param.21) | copy-start | bytes 393220
  138.7 23.3 %copy-start.16 = (bf16[8,32,1536]{2,1,0:T(8,128)(2,1)S(1)}, bf16[8,32,1536]{2,1,0:T(8,128)(2,1)}, u32[]{:S(2)}) copy-start(bf16[8,32,1536]{2,1,0:T(8,128)(2,1)} %get-tuple-element.22) | copy-start | bytes 2359300
  138.7 23.3 %copy-start.20 = (f32[256,256]{1,0:T(8,128)S(1)}, f32[256,256]{1,0:T(8,128)}, u32[]{:S(2)}) copy-start(f32[256,256]{1,0:T(8,128)} %get-tuple-element.47) | copy-start | bytes 786436
  139.7 24.7 %copy-start.8 = (bf16[256,256]{1,0:T(8,128)(2,1)S(1)}, bf16[256,256]{1,0:T(8,128)(2,1)}, u32[]{:S(2)}) copy-start(bf16[256,256]{1,0:T(8,128)(2,1)} %copy-done.7) | copy-start | bytes 393220
  162.0 2.5 %copy-start.11 = (bf16[8,32,256]{2,1,0:T(8,128)(2,1)S(1)}, bf16[8,32,256]{2,1,0:T(8,128)(2,1)}, u32[]{:S(2)}) copy-start(bf16[8,32,256]{2,1,0:T(8,128)(2,1)} %get-tuple-element.35) | copy-start | bytes 393220
  164.5 19.0 %copy-start.9 = (bf16[4,32,2048]{2,1,0:T(8,128)(2,1)S(1)}, bf16[4,32,2048]{2,1,0:T(8,128)(2,1)}, u32[]{:S(2)}) copy-start(bf16[4,32,2048]{2,1,0:T(8,128)(2,1)} %get-tuple-element.38) | copy-start | bytes 1572868
  164.5 19.0 %copy-start.10 = (bf16[4,32,2048]{2,1,0:T(8,128)(2,1)S(1)}, bf16[4,32,2048]{2,1,0:T(8,128)(2,1)}, u32[]{:S(2)}) copy-start(bf16[4,32,2048]{2,1,0:T(8,128)(2,1)} %get-tuple-element.39) | copy-start | bytes 1572868
